TPU v7x, 128 devices: a whole 4x4x4 slice. The times are simulated.
128 devices in a mesh: depth: 8 (over y, core), seg: 16 (over z, x).
Axes of the slice: x: 4, y: 4, z: 4, core: 2. Of those that a mesh axis runs over, the one named last changes fastest.
Arguments:
- queries: bfloat16 [8, 16, 128, 2560], P('depth', 'seg'), may hold values from -6 to 6, as said below
- keys_values: bfloat16 [8, 16, 2, 128, 512], P('depth', 'seg'), may hold values from -6 to 6
- grad_out: bfloat16 [8, 16, 128, 2560], P('depth', 'seg'), may hold values from -6 to 6
- parents: int32 [7, 16, 1], replicated, may hold values from 0 to 15
Outputs:
- grad_queries: bfloat16 [8, 16, 128, 2560], P('depth', 'seg')
- grad_keys_values: bfloat16 [8, 16, 2, 128, 512], P('depth', 'seg')
Inputs may be any that keep to these rules, and one draw needn't show every extreme that they name: `queries`: a few query rows and key rows may be nearly parallel in some draws. `parents`: every column of a level is somebody's parent in some level.
All inputs are finite; a program needn't handle non-finite values.
Results may differ from a plain program's by a relative error of at most 0.012.
Values may be sent and summed in bfloat16 or wider, within the bound.
A program may use at most 128 MiB of HBM per device.

v0:
```python
import functools

import jax
import jax.numpy as jnp
from jax import lax
from jax.experimental import pallas as pl
from jax.experimental.pallas import tpu as pltpu
from jax.sharding import PartitionSpec as P

HEADS = 20
KV_HEADS = 4
HEAD_DIM = 128
GROUP = HEADS // KV_HEADS
ROWS = 128
LEVELS = 8
SEGS = 16
PIECE = 16
PIECES_PER_PART = ROWS // PIECE
STACK = GROUP * ROWS
PAIR = 2 * ROWS
LAG = 2

NEG_FILL = -1e30
SCALE = HEAD_DIM ** -0.5
EXP2_SCALE = SCALE * 1.4426950408889634
MESH = pl.DeviceIdType.MESH
BF16 = jnp.bfloat16
F32 = jnp.float32

PLANE = ((0, 1, 2, 3), (3, 1, 2, 0))

LIFTS = (
    (0, 0, 0, 0, ("above", "below"), True),
    (0, 1, 0, 1, ("above",), True),
    (0, 2, 0, 2, ("above",), True),
    (0, 3, 0, 3, (), True),
    (0, 1, 1, 0, ("above",), True),
    (0, 2, 1, 1, ("above",), True),
    (0, 3, 1, 2, (), True),
    (0, 3, 1, 0, (), True),
    (0, 2, 2, 0, (), True),
    (0, 3, 2, 1, (), True),
    (1, 3, 0, 0, ("above", "below"), True),
    (1, 1, 0, 1, ("above", "below"), True),
    (1, 2, 0, 2, ("below",), True),
    (1, 0, 0, 3, (), True),
    (1, 2, 1, 0, ("below",), True),
    (1, 2, 1, 1, (), True),
    (1, 1, 1, 2, ("below",), False),
    (1, 0, 1, 0, (), True),
    (1, 0, 1, 1, (), True),
    (1, 1, 2, 0, (), True),
    (1, 0, 2, 2, (), True),
)

CHAIN = (
    (0, 3, 0, 2, None, 0, "below"),
    (0, 3, 0, 1, None, 1, "below"),
    (0, 3, 0, 0, None, 2, "above"),
    (0, 2, 0, 0, None, 1, "below"),
    (0, 2, 1, 1, 1, 0, "below"),
    (0, 1, 1, 0, 1, 0, "below"),
    (1, 0, 0, 0, None, 2, "below"),
    (1, 0, 0, 1, None, 0, "above"),
    (1, 0, 0, 2, None, 1, "above"),
    (1, 2, 0, 1, None, 2, "below"),
    (1, 1, 0, 0, None, 1, "above"),
    (1, 2, 1, 0, 1, 0, "above"),
    (1, 1, 1, None, 1, 0, "above"),
)

TOTALS = (
    (0, 0, (0, 2)), (0, 1, (0,)), (0, 2, (0,)),
    (1, 1, (0, 2)), (1, 2, (0,)), (1, 3, (0, 2)),
)


def lanes(index, count=1):
    width = count * HEAD_DIM
    return pl.ds(pl.multiple_of(index * width, width), width)


def rows_of(index, count):
    return pl.ds(pl.multiple_of(index * count, count), count)


def piece_of(index):
    return index // PIECES_PER_PART, rows_of(index % PIECES_PER_PART, PIECE)


def fold(tile):
    return tile.reshape(tile.shape[0] // 8, 8, tile.shape[1])


def kernel(
    parents, queries, keys_values, grad_out, grad_queries, grad_kv,
    anc, pick, spread, pieces, chosen, blocks, terms, term_pieces, own, own_out, own_in,
    stacks, staged, query_sum, stats, logits, grad_probs, probs, grad_logits,
    kept, total_sum, cross_out, cross_in, chain_out, chain_in, final_out, final_in,
    p1_send, p1_recv, up_send, up_recv, q_send, q_recv, k_send, k_recv, p3_send, p3_recv,
    b1_send, b1_recv, o_send, o_recv, d_send, d_recv, x_send, x_recv, c_send, c_recv,
    f_send, f_recv,
):
    level = lax.axis_index("depth")
    me = lax.axis_index("seg")
    y = level // 2
    core = level % 2
    places = {
        "sibling": 2 * y + 1 - core,
        "above": 2 * ((y + 1) % 4) + core,
        "below": 2 * ((y + 3) % 4) + core,
    }
    sibling = places["sibling"]
    outer = (y == 0) | (y == 3)
    partner = jnp.where(outer, 2 * (3 - y) + core, level)

    def host_of(head):
        return jnp.where(head % 2 == 1, partner, level)

    def remote(src, dst, send_sem, recv_sem, device):
        return pltpu.make_async_remote_copy(
            src_ref=src, dst_ref=dst, send_sem=send_sem, recv_sem=recv_sem,
            device_id=device, device_id_type=MESH,
        )

    def wait_bytes(ref, sem):
        pltpu.make_async_copy(ref, ref, sem).wait()

    def per_level(which, action):
        for count in range(1, LEVELS):
            pl.when(which == count)(functools.partial(action, count))

    def move(head, src, dst, send_sem, recv_sem):
        host = host_of(head)

        @pl.when(host != level)
        def _():
            remote(src, dst, send_sem, recv_sem, (host, me)).start()

        @pl.when(host == level)
        def _():
            pltpu.make_async_copy(src, dst, recv_sem).start()

    barrier = pltpu.get_barrier_semaphore()

    def greet(device):
        pl.semaphore_signal(barrier, inc=1, device_id=device, device_id_type=MESH)

    @pl.loop(1, SEGS)
    def _(step):
        greet((level, (me + step) % SEGS))

    for other in places.values():
        greet((other, me))

    @pl.when(outer)
    def _():
        @pl.loop(0, SEGS)
        def _(step):
            greet((partner, (me + step) % SEGS))

    pl.semaphore_wait(barrier, SEGS - 1 + 3 + jnp.where(outer, SEGS, 0))

    @pl.loop(0, KV_HEADS)
    def _(head):
        host = host_of(head)

        def source(peer):
            part, span = piece_of(peer)
            return keys_values.at[0, 0, part, span, lanes(head)]

        @pl.loop(1, SEGS)
        def _(step):
            peer = (me + step) % SEGS
            remote(
                source(peer), pieces.at[head, level, me],
                p1_send.at[head], p1_recv.at[head], (host, peer),
            ).start()

        @pl.when(host != level)
        def _():
            remote(
                source(me), pieces.at[head, level, me],
                p1_send.at[head], p1_recv.at[head], (host, me),
            ).start()

        @pl.when(host == level)
        def _():
            pltpu.make_async_copy(
                source(me), pieces.at[head, level, me], p1_recv.at[head]
            ).start()

    def move_inputs(head):
        move(
            head, keys_values.at[0, 0, :, :, lanes(head)], blocks.at[head, 0],
            k_send.at[head], k_recv.at[head],
        )

        @pl.loop(0, GROUP)
        def _(group):
            for index, array in enumerate((queries, grad_out)):
                move(
                    head, array.at[0, 0, :, lanes(head * GROUP + group)],
                    stacks.at[head, index, rows_of(group, ROWS), :],
                    q_send.at[head], q_recv.at[head],
                )

    @pl.loop(0, 2)
    def _(parity):
        target_level = host_of(parity)

        @pl.loop(0, SEGS)
        def _(column):
            current = column
            for offset in range(1, LEVELS):
                current = parents[jnp.maximum(target_level - offset, 0), 0, current]
                anc[parity, offset, column] = current

        @pl.loop(1, LEVELS)
        def _(offset):
            lane = lax.broadcasted_iota(jnp.int32, (PIECE, SEGS * PIECE), 1)
            row = lax.broadcasted_iota(jnp.int32, (PIECE, SEGS * PIECE), 0)
            target = lane % PIECE
            lane_column = lane // PIECE
            for column in range(SEGS):
                found = anc[parity, offset, column] * PIECE
                pick[parity, offset, rows_of(column, PIECE), :] = jnp.where(
                    lane == found + row, 1.0, 0.0
                ).astype(BF16)
                target = target + jnp.where(lane_column == column, found, 0)
            for column in range(SEGS):
                spread[parity, offset, rows_of(column, PIECE), :] = jnp.where(
                    target == row + column * PIECE, 1.0, 0.0
                ).astype(BF16)

    @pl.loop(0, KV_HEADS)
    def _(head):
        here = host_of(head)

        @pl.when(here % 2 == 0)
        def _():
            blocks[head, here + 1] = jnp.zeros((2, ROWS, HEAD_DIM), BF16)

    def lift_copies(head, entry):
        parity, row, stage, plane, targets, to_sibling = entry
        which = 2 * plane + core
        copies = []
        slots = {"above": 0, "below": 1} if stage == 0 else {"above": 2, "below": 2}
        for target in targets:
            copies.append((slots[target], None, places[target]))
        if to_sibling:
            copies.append((3 + plane, core == 0 if stage == 0 else None, sibling))
        return [
            (
                condition,
                remote(
                    pieces.at[head, which], pieces.at[head, which],
                    up_send.at[head, slot], up_recv.at[head, which], (device, me),
                ),
            )
            for slot, condition, device in copies
        ]

    def each_lift(head, stages, action):
        for entry in LIFTS:
            if entry[2] in stages:
                pl.when((head % 2 == entry[0]) & (y == entry[1]))(
                    functools.partial(action, entry)
                )

    def lift_stage(head, stage):
        def forward(entry):
            if stage > 0:
                which = 2 * entry[3] + core
                wait_bytes(pieces.at[head, which], up_recv.at[head, which])
            for condition, copy in lift_copies(head, entry):
                if condition is None:
                    copy.start()
                else:
                    pl.when(condition)(copy.start)

        each_lift(head, (stage,), forward)

    @pl.loop(0, KV_HEADS)
    def _(head):
        here = host_of(head)
        wait_bytes(pieces.at[head, here], p1_recv.at[head])
        lift_stage(head, 0)
        move_inputs(head)

    def select(head):
        here = host_of(head)
        parity = head % 2

        @pl.loop(0, 4)
        def _(plane):
            other = 2 * plane + 1 - core

            @pl.when(other < here)
            def _():
                wait_bytes(pieces.at[head, other], up_recv.at[head, other])

        def pick_up(last):
            for offset in range(1, last + 1):
                found = jnp.dot(
                    pick[parity, offset],
                    pieces[head, jnp.maximum(here - offset, 0)].reshape(SEGS * PIECE, HEAD_DIM),
                    preferred_element_type=F32,
                )
                chosen[head, :, offset - 1] = found.astype(BF16).reshape(SEGS, PIECE, HEAD_DIM)

        pl.when((here > 0) & (here < 4))(lambda: pick_up(3))
        pl.when(here >= 4)(lambda: pick_up(7))

        def send(count):
            part, span = piece_of(me)

            @pl.loop(1, SEGS)
            def _(step):
                peer = (me + step) % SEGS
                remote(
                    chosen.at[head, peer, pl.ds(0, count)],
                    blocks.at[head, pl.ds(1, count), part, span, :],
                    p3_send.at[head], p3_recv.at[head], (level, peer),
                ).start()

            pltpu.make_async_copy(
                chosen.at[head, me, pl.ds(0, count)],
                blocks.at[head, pl.ds(1, count), part, span, :], p3_recv.at[head],
            ).start()

        per_level(here, send)

    def attend(head):
        here = host_of(head)
        pairs = here // 2 + 1
        contract_last = (((1,), (1,)), ((), ()))
        span_all = [pl.ds(group * ROWS, ROWS) for group in range(GROUP)]

        def block_pair(pair, part):
            return blocks[head, pl.ds(2 * pair, 2), part].reshape(PAIR, HEAD_DIM)

        stats[0] = jnp.full((8, STACK), NEG_FILL, F32)

        @pl.loop(0, pairs)
        def _(pair):
            span_rows = rows_of(pair, PAIR)
            logits[span_rows, :] = lax.dot_general(
                block_pair(pair, 0), stacks[head, 0], contract_last, preferred_element_type=F32
            )
            grad_probs[span_rows, :] = lax.dot_general(
                block_pair(pair, 1), stacks[head, 1], contract_last, preferred_element_type=F32
            )

            @pl.when(pair == 0)
            def _():
                u_row = lax.broadcasted_iota(jnp.int32, (ROWS, ROWS), 0)
                t_row = lax.broadcasted_iota(jnp.int32, (ROWS, ROWS), 1)
                for span in span_all:
                    logits[0:ROWS, span] = jnp.where(
                        u_row <= t_row, logits[0:ROWS, span], NEG_FILL
                    )

            @pl.when((pair == pairs - 1) & (here % 2 == 0))
            def _():
                logits[rows_of(here + 1, ROWS), :] = jnp.full((ROWS, STACK), NEG_FILL, F32)

            for span in span_all:
                stats[0, :, span] = jnp.maximum(
                    stats[0, :, span], fold(logits[span_rows, span]).max(0)
                )

        stats[1] = jnp.zeros((8, STACK), F32)
        stats[2] = jnp.zeros((8, STACK), F32)
        stats[0] = jnp.broadcast_to(stats[0].max(0, keepdims=True), (8, STACK))

        @pl.loop(0, pairs)
        def _(pair):
            span_rows = rows_of(pair, PAIR)
            for span in span_all:
                top = stats[0, 0:1, span]
                tile = jnp.exp2((logits[span_rows, span] - top) * EXP2_SCALE)
                logits[span_rows, span] = tile
                stats[1, :, span] += fold(tile).sum(0)
                stats[2, :, span] += fold(tile * grad_probs[span_rows, span]).sum(0)

        inverse = 1.0 / stats[1].sum(0, keepdims=True)
        delta = stats[2].sum(0, keepdims=True) * inverse
        stats[1] = jnp.broadcast_to(inverse, (8, STACK))
        stats[2] = jnp.broadcast_to(delta, (8, STACK))
        query_sum[...] = jnp.zeros((HEAD_DIM, STACK), F32)

        @pl.loop(0, pairs)
        def _(pair):
            span_rows = rows_of(pair, PAIR)
            for span in span_all:
                exact = logits[span_rows, span] * stats[1, 0:1, span]
                probs[:, span] = exact.astype(BF16)
                grad_logits[:, span] = (
                    exact * (grad_probs[span_rows, span] - stats[2, 0:1, span])
                ).astype(BF16)
            value_term = jnp.dot(probs[...], stacks[head, 1], preferred_element_type=F32)
            key_term = SCALE * jnp.dot(
                grad_logits[...], stacks[head, 0], preferred_element_type=F32
            )
            for part, term in enumerate((key_term, value_term)):
                terms[head, pl.ds(2 * pair, 2), part] = term.astype(BF16).reshape(
                    2, ROWS, HEAD_DIM
                )

                @pl.when(pair == 0)
                def _():
                    own[head, part] = term[0:ROWS]

            query_sum[...] += lax.dot_general(
                block_pair(pair, 0), grad_logits[...], (((0,), (0,)), ((), ())),
                preferred_element_type=F32,
            )

        for group, span in enumerate(span_all):
            staged[head, :, span] = (SCALE * query_sum[:, span].T).astype(BF16)

    def staged_copy_target(head):
        return grad_queries.at[0, 0, :, lanes(head, GROUP)]

    def send_results(head):
        host = host_of(head)
        here = host

        def send(count):
            @pl.loop(1, SEGS)
            def _(step):
                peer = (me + step) % SEGS
                part, span = piece_of(peer)
                remote(
                    terms.at[head, pl.ds(1, count), part, span, :],
                    term_pieces.at[head, pl.ds(1, count), me],
                    b1_send.at[head], b1_recv.at[head], (level, peer),
                ).start()

            part, span = piece_of(me)
            pltpu.make_async_copy(
                terms.at[head, pl.ds(1, count), part, span, :],
                term_pieces.at[head, pl.ds(1, count), me], b1_recv.at[head],
            ).start()

        per_level(here, send)
        move(
            head, staged.at[head], staged_copy_target(head), d_send.at[head], d_recv.at[head]
        )

        @pl.when(host != level)
        def _():
            own_out[head] = own[head].astype(BF16)
            remote(
                own_out.at[head], own_in.at[head], o_send.at[head], o_recv.at[head], (host, me)
            ).start()

    def summed(head, offset):
        return jnp.dot(
            spread[head % 2, offset],
            term_pieces[head, offset].reshape(SEGS * PIECE, HEAD_DIM),
            preferred_element_type=F32,
        )

    def cross_copy(head, plane):
        return remote(
            cross_out.at[head, plane], cross_in.at[head, plane],
            x_send.at[head, plane], x_recv.at[head, plane], (sibling, me),
        )

    def sum_stage(head):
        here = host_of(head)
        per_level(
            here,
            lambda count: wait_bytes(term_pieces.at[head, pl.ds(1, count)], b1_recv.at[head]),
        )

        def sums(planes):
            for plane in range(planes):
                offset = jnp.maximum(here - (2 * plane + 1 - core), 1)
                cross_out[head, plane] = summed(head, offset).astype(BF16)
            for plane in range(planes - 1):
                offset = jnp.maximum(here - (2 * plane + core), 1)
                kept[head, plane] = summed(head, offset)

        pl.when((here > 0) & (here < 4))(lambda: sums(2))
        pl.when(here >= 4)(lambda: sums(4))

        @pl.loop(0, 4)
        def _(plane):
            @pl.when(here - (2 * plane + 1 - core) >= 1)
            def _():
                cross_copy(head, plane).start()

    def chain_copy(head, entry):
        added, slot, place = entry[4:]
        source = chain_in.at[head, added] if entry[3] is None else chain_out.at[head, slot]
        return remote(
            source, chain_in.at[head, slot], c_send.at[head, slot], c_recv.at[head, slot],
            (places[place], me),
        )

    def each_chain(head, stages, action):
        for entry in CHAIN:
            if entry[2] in stages:
                pl.when((head % 2 == entry[0]) & (y == entry[1]))(
                    functools.partial(action, entry)
                )

    def chain_stage(head, stage):
        def send(entry):
            plane, added, slot = entry[3:6]
            if added is not None:
                wait_bytes(chain_in.at[head, added], c_recv.at[head, added])
            if plane is not None:
                value = kept[head, plane]
                if added is not None:
                    value = value + chain_in[head, added].astype(F32)
                chain_out[head, slot] = value.astype(BF16)
            chain_copy(head, entry).start()

        each_chain(head, (stage,), send)

    def chain_first(head):
        plane_here = host_of(head) // 2

        @pl.loop(0, plane_here - core + 1)
        def _(plane):
            wait_bytes(cross_in.at[head, plane], x_recv.at[head, plane])

        @pl.loop(0, plane_here)
        def _(plane):
            kept[head, plane] += cross_in[head, plane].astype(F32)

        chain_stage(head, 0)

    def chain_second(head):
        chain_stage(head, 1)

    def final_send(head):
        host = host_of(head)

        @pl.when(host < LEVELS - 1)
        def _():
            total_sum[...] = jnp.zeros((SEGS * PIECE, HEAD_DIM), F32)

            def add(slots):
                for slot in slots:
                    wait_bytes(chain_in.at[head, slot], c_recv.at[head, slot])
                    total_sum[...] += chain_in[head, slot].astype(F32)

            for parity, row, slots in TOTALS:
                pl.when((head % 2 == parity) & (y == row))(functools.partial(add, slots))

            @pl.when(core == 0)
            def _():
                total_sum[...] += cross_in[head, host // 2].astype(F32)

            final_out[head] = total_sum[...].astype(BF16).reshape(SEGS, PIECE, HEAD_DIM)
            part, span = piece_of(me)

            @pl.loop(1, SEGS)
            def _(step):
                peer = (me + step) % SEGS
                remote(
                    final_out.at[head, peer], final_in.at[head, part, span, :],
                    f_send.at[head], f_recv.at[head], (host, peer),
                ).start()

            move(
                head, final_out.at[head, me], final_in.at[head, part, span, :],
                f_send.at[head], f_recv.at[head],
            )

    def final_store(head):
        away = host_of(head) != level

        @pl.when(away)
        def _():
            wait_bytes(own_in.at[head], o_recv.at[head])
            own[head] = own_in[head].astype(F32)

        @pl.when(level < LEVELS - 1)
        def _():
            wait_bytes(final_in.at[head], f_recv.at[head])
            own[head] = own[head] + final_in[head].astype(F32)

        grad_kv[0, 0, :, :, lanes(head)] = own[head].astype(BF16)

    stages = (sum_stage, chain_first, chain_second, final_send, final_store)

    @pl.loop(0, KV_HEADS + LAG + len(stages))
    def _(tick):
        @pl.when(tick < KV_HEADS)
        def _():
            lift_stage(tick, 1)

        @pl.when((tick >= 1) & (tick < KV_HEADS + 1))
        def _():
            select(tick - 1)

        @pl.when(tick < KV_HEADS)
        def _():
            lift_stage(tick, 2)

        @pl.when((tick >= LAG) & (tick < KV_HEADS + LAG))
        def _():
            head = tick - LAG
            per_level(
                host_of(head),
                lambda count: wait_bytes(blocks.at[head, pl.ds(1, count)], p3_recv.at[head]),
            )
            wait_bytes(blocks.at[head, 0], k_recv.at[head])
            wait_bytes(stacks.at[head], q_recv.at[head])
            attend(head)
            send_results(head)

        for lag, stage in enumerate(stages, LAG + 1):
            @pl.when((tick >= lag) & (tick < KV_HEADS + lag))
            def _():
                stage(tick - lag)

    @pl.loop(0, KV_HEADS)
    def _(head):
        host = host_of(head)
        away = host != level
        wait_bytes(staged_copy_target(head), d_recv.at[head])
        wait_bytes(final_out.at[head, pl.ds(1, SEGS - 1)], p1_send.at[head])

        @pl.when(away)
        def _():
            wait_bytes(final_out.at[head, 0], p1_send.at[head])
            wait_bytes(blocks.at[head, 0], k_send.at[head])
            wait_bytes(stacks.at[head], q_send.at[head])
            wait_bytes(staged.at[head], d_send.at[head])
            wait_bytes(own_out.at[head], o_send.at[head])

        def lifted(entry):
            for condition, copy in lift_copies(head, entry):
                if condition is None:
                    copy.wait_send()
                else:
                    pl.when(condition)(copy.wait_send)

        each_lift(head, (0, 1, 2), lifted)

        def sent(count):
            wait_bytes(chosen.at[head, pl.ds(1, SEGS - 1), pl.ds(0, count)], p3_send.at[head])
            wait_bytes(
                term_pieces.at[head, pl.ds(1, count), pl.ds(1, SEGS - 1)], b1_send.at[head]
            )

        per_level(host, sent)

        @pl.loop(0, 4)
        def _(plane):
            @pl.when(host - (2 * plane + 1 - core) >= 1)
            def _():
                cross_copy(head, plane).wait_send()

        each_chain(head, (0, 1), lambda entry: chain_copy(head, entry).wait_send())

        @pl.when(host < LEVELS - 1)
        def _():
            wait_bytes(final_out.at[head, pl.ds(1, SEGS - 1)], f_send.at[head])

            @pl.when(away)
            def _():
                wait_bytes(final_out.at[head, 0], f_send.at[head])


def shards(queries, keys_values, grad_out, parents):
    vmem = pl.BlockSpec(memory_space=pltpu.VMEM)
    smem = pl.BlockSpec(memory_space=pltpu.SMEM)
    anywhere = pl.BlockSpec(memory_space=pl.ANY)
    dma = pltpu.SemaphoreType.DMA
    tile = (SEGS, PIECE, HEAD_DIM)
    flat = (SEGS * PIECE, HEAD_DIM)
    keys_count = LEVELS * ROWS
    part_pair = (2, ROWS, HEAD_DIM)
    selectors = (2, LEVELS, SEGS * PIECE, SEGS * PIECE)
    scratch = [
        pltpu.SMEM((2, LEVELS, SEGS), jnp.int32),
        pltpu.VMEM(selectors, BF16),
        pltpu.VMEM(selectors, BF16),
        pltpu.VMEM((KV_HEADS, LEVELS) + tile, BF16),
        pltpu.VMEM((KV_HEADS, SEGS, LEVELS - 1, PIECE, HEAD_DIM), BF16),
        pltpu.VMEM((KV_HEADS, LEVELS) + part_pair, BF16),
        pltpu.VMEM((KV_HEADS, LEVELS) + part_pair, BF16),
        pltpu.VMEM((KV_HEADS, LEVELS) + tile, BF16),
        pltpu.VMEM((KV_HEADS,) + part_pair, F32),
        pltpu.VMEM((KV_HEADS,) + part_pair, BF16),
        pltpu.VMEM((KV_HEADS,) + part_pair, BF16),
        pltpu.VMEM((KV_HEADS, 2, STACK, HEAD_DIM), BF16),
        pltpu.VMEM((KV_HEADS, ROWS, STACK), BF16),
        pltpu.VMEM((HEAD_DIM, STACK), F32),
        pltpu.VMEM((3, 8, STACK), F32),
        pltpu.VMEM((keys_count, STACK), F32),
        pltpu.VMEM((keys_count, STACK), F32),
        pltpu.VMEM((PAIR, STACK), BF16),
        pltpu.VMEM((PAIR, STACK), BF16),
        pltpu.VMEM((KV_HEADS, 3) + flat, F32),
        pltpu.VMEM(flat, F32),
        pltpu.VMEM((KV_HEADS, 4) + flat, BF16),
        pltpu.VMEM((KV_HEADS, 4) + flat, BF16),
        pltpu.VMEM((KV_HEADS, 3) + flat, BF16),
        pltpu.VMEM((KV_HEADS, 3) + flat, BF16),
        pltpu.VMEM((KV_HEADS,) + tile, BF16),
        pltpu.VMEM((KV_HEADS,) + part_pair, BF16),
        dma((KV_HEADS,)), dma((KV_HEADS,)),
        dma((KV_HEADS, 7)), dma((KV_HEADS, LEVELS)),
        dma((KV_HEADS,)), dma((KV_HEADS,)),
        dma((KV_HEADS,)), dma((KV_HEADS,)),
        dma((KV_HEADS,)), dma((KV_HEADS,)),
        dma((KV_HEADS,)), dma((KV_HEADS,)),
        dma((KV_HEADS,)), dma((KV_HEADS,)),
        dma((KV_HEADS,)), dma((KV_HEADS,)),
        dma((KV_HEADS, 4)), dma((KV_HEADS, 4)),
        dma((KV_HEADS, 3)), dma((KV_HEADS, 3)),
        dma((KV_HEADS,)), dma((KV_HEADS,)),
    ]
    return pl.pallas_call(
        kernel,
        out_shape=(
            jax.ShapeDtypeStruct(queries.shape, BF16),
            jax.ShapeDtypeStruct(keys_values.shape, BF16),
        ),
        in_specs=[smem, anywhere, anywhere, anywhere],
        out_specs=(anywhere, vmem),
        scratch_shapes=scratch,
        compiler_params=pltpu.CompilerParams(
            collective_id=0, has_side_effects=True, vmem_limit_bytes=56 * 1024 * 1024
        ),
        cost_estimate=pl.CostEstimate(
            flops=5 * 2 * HEADS * LEVELS * ROWS * ROWS * HEAD_DIM,
            bytes_accessed=8 * 1024 * 1024,
            transcendentals=HEADS * LEVELS * ROWS * ROWS,
        ),
    )(parents.transpose(0, 2, 1), queries, keys_values, grad_out)


def solution(mesh):
    in_specs = (
        P("depth", "seg", None, None),
        P("depth", "seg", None, None, None),
        P("depth", "seg", None, None),
        P(),
    )
    out_specs = (P("depth", "seg", None, None), P("depth", "seg", None, None, None))
    return jax.shard_map(shards, mesh=mesh, in_specs=in_specs, out_specs=out_specs, check_vma=False)
```

profile of v0, /device:TPU:0, one launch (start us, length us, event | category | flops | bytes accessed | tf_op | source)
XLA Modules:
  0.0 82.9 jit_solution(10798757920567834212)
XLA Ops:
  0.6 79.6 %shard_map.59 = (bf16[1,1,128,2560]{3,2,1,0:T(8,128)(2,1)}, bf16[1,1,2,128,512]{4,3,2,1,0:T(8,128)(2,1)}) custom-call(s32[7,1,16]{2,1,0:T(1,128)} %bitcast.1, bf16[1,1,128,2560]{3,2,1,0:T(8,128)(2,1)} %queries.1, bf16[1,1,2,128,512]{4,3,2,1,0:T(8,128)(2,1)} %keys_values.1, bf16[1,1,128,2560]{3,2,1,0:T(8,128)(2,1)} %grad_out.1), custom_call_target="tpu_custom_call" | custom-call | flops 3355443200 | bytes 8388608 | tf_op jit(solution)/shard_map/pallas_call | solution.py:723
  80.2 0.0 copy-start
  80.2 2.0 %copy.8 = bf16[1,1,128,2560]{3,2,1,0:T(8,128)(2,1)} copy(bf16[1,1,128,2560]{3,2,1,0:T(8,128)(2,1)} %get-tuple-element.4) | data formatting | bytes 1310720
  82.2 0.0 copy-done
  82.2 0.7 copy.9
Async XLA Ops:
  80.2 2.0 %copy-start = (bf16[1,1,2,128,512]{4,3,2,1,0:T(8,128)(2,1)S(1)}, bf16[1,1,2,128,512]{4,3,2,1,0:T(8,128)(2,1)}, u32[]{:S(2)}) copy-start(bf16[1,1,2,128,512]{4,3,2,1,0:T(8,128)(2,1)} %get-tuple-element.5) | copy-start | bytes 786436
where the time goes:
time: 83.3 us; the launch traced here: 82.9 us
  Pallas kernels  79.6 us (96%)
  local copies, waits for them, and re-layouts  2.71 us (3%)
    pallas_call x1, Pallas kernels, shards(): pl.pallas_call(kernel, out_shape=(jax.ShapeDtypeStruct(queries.shape, BF1...  79.6 us
    unnamed x4, local copies, waits for them, and re-layouts  2.71 us

commit v1 on v0

v1 whole, which is shorter than its diff:
```python
import functools

import jax
import jax.numpy as jnp
from jax import lax
from jax.experimental import pallas as pl
from jax.experimental.pallas import tpu as pltpu
from jax.sharding import PartitionSpec as P

HEADS = 20
KV_HEADS = 4
HEAD_DIM = 128
GROUP = HEADS // KV_HEADS
ROWS = 128
LEVELS = 8
SEGS = 16
PIECE = 16
PIECES_PER_PART = ROWS // PIECE
STACK = GROUP * ROWS
PAIR = 2 * ROWS
LAG = 2

NEG_FILL = -1e30
SCALE = HEAD_DIM ** -0.5
EXP2_SCALE = SCALE * 1.4426950408889634
MESH = pl.DeviceIdType.MESH
BF16 = jnp.bfloat16
F32 = jnp.float32


def half(value):
    return lax.div(value, 2)


def odd(value):
    return lax.rem(value, 2)


def name_of(head):
    return 2 * odd(head) + half(head)


def wrapped(index):
    return jnp.where(index >= SEGS, index - SEGS, index)


def lanes(index, count=1):
    width = count * HEAD_DIM
    return pl.ds(pl.multiple_of(index * width, width), width)


def rows_of(index, count):
    return pl.ds(pl.multiple_of(index * count, count), count)


def piece_of(index):
    part = jnp.where(index >= PIECES_PER_PART, 1, 0)
    return part, rows_of(index - part * PIECES_PER_PART, PIECE)


def fold(tile):
    return tile.reshape(tile.shape[0] // 8, 8, tile.shape[1])


def kernel(
    parents, queries, keys_values, grad_out, grad_queries, grad_kv,
    anc, pick, spread, pieces, chosen, blocks, terms, term_pieces, own, own_out, own_in,
    inputs, stacks, staged, query_sum, stats, logits, grad_probs, probs, grad_logits,
    kept, total_sum, cross_out, cross_in, climb_out, climb_in, final_out, final_in,
    p1_send, p1_recv, up_send, up_recv, q_send, q_recv, k_send, k_recv, p3_send, p3_recv,
    b1_send, b1_recv, o_send, o_recv, d_send, d_recv, x_send, x_recv, c_send, c_recv,
    f_send, f_recv,
):
    level = lax.axis_index("depth")
    me = lax.axis_index("seg")
    y = half(level)
    core = odd(level)
    sibling = 2 * y + 1 - core
    outer = (y == 0) | (y == 3)
    partner = jnp.where(outer, 2 * (3 - y) + core, level)

    def host_of(head):
        return jnp.where(odd(head) == 1, partner, level)

    def device_of(head, plane):
        swapped = (odd(head) == 1) & ((plane == 0) | (plane == 3))
        return 2 * jnp.where(swapped, 3 - plane, plane) + core

    def remote(src, dst, send_sem, recv_sem, device):
        return pltpu.make_async_remote_copy(
            src_ref=src, dst_ref=dst, send_sem=send_sem, recv_sem=recv_sem,
            device_id=device, device_id_type=MESH,
        )

    def wait_bytes(ref, sem):
        pltpu.make_async_copy(ref, ref, sem).wait()

    def per_plane(which, action):
        for plane in range(LEVELS // 2):
            pl.when((which > 0) & (half(which) == plane))(
                functools.partial(action, 2 * plane + 1)
            )

    def move(head, src, dst, send_sem, recv_sem):
        host = host_of(head)

        @pl.when(host != level)
        def _():
            remote(src, dst, send_sem, recv_sem, (host, me)).start()

        @pl.when(host == level)
        def _():
            pltpu.make_async_copy(src, dst, recv_sem).start()

    barrier = pltpu.get_barrier_semaphore()

    def greet(device):
        pl.semaphore_signal(barrier, inc=1, device_id=device, device_id_type=MESH)

    @pl.loop(1, SEGS)
    def _(step):
        greet((level, wrapped(me + step)))

    greet((sibling, me))
    for step in range(1, 4):
        greet((lax.rem(level + 2 * step, LEVELS), me))

    @pl.when(outer)
    def _():
        @pl.loop(0, SEGS)
        def _(step):
            greet((partner, wrapped(me + step)))

    pl.semaphore_wait(barrier, SEGS - 1 + 4 + jnp.where(outer, SEGS, 0))

    @pl.loop(0, 2)
    def _(group):
        host = host_of(group)

        def source(peer):
            part, span = piece_of(peer)
            return keys_values.at[0, 0, part, span, lanes(group, 2)]

        @pl.loop(1, SEGS)
        def _(step):
            peer = wrapped(me + step)
            remote(
                source(peer), pieces.at[group, level, me],
                p1_send.at[group], p1_recv.at[group], (host, peer),
            ).start()

        @pl.when(host != level)
        def _():
            remote(
                source(me), pieces.at[group, level, me],
                p1_send.at[group], p1_recv.at[group], (host, me),
            ).start()

        @pl.when(host == level)
        def _():
            pltpu.make_async_copy(
                source(me), pieces.at[group, level, me], p1_recv.at[group]
            ).start()

    def move_inputs(head):
        name = name_of(head)
        move(
            head, keys_values.at[0, 0, :, :, lanes(name)], blocks.at[head, 0],
            k_send.at[head], k_recv.at[head],
        )
        for index, array in enumerate((queries, grad_out)):
            move(
                head, array.at[0, 0, :, lanes(name, GROUP)], inputs.at[head, index],
                q_send.at[head], q_recv.at[head],
            )

    def unit(head, which):
        return pieces.at[odd(head), which, :, :, lanes(half(head))]

    def lift(head, which, slot, device):
        return remote(
            unit(head, which), unit(head, which),
            up_send.at[head, slot], up_recv.at[head, which], (device, me),
        )

    def own_lifts(head, action):
        here = host_of(head)
        plane = half(here)
        for step in range(1, 4):
            @pl.when(plane + step <= 3)
            def _():
                action(lift(head, here, step - 1, device_of(head, plane + step)))

        @pl.when(core == 0)
        def _():
            action(lift(head, here, 3, sibling))

    def passed_on(head, action):
        @pl.loop(0, half(host_of(head)))
        def _(plane):
            action(2 * plane + core, lift(head, 2 * plane + core, 4 + plane, sibling))

    for group in range(2):
        here = host_of(group)
        wait_bytes(pieces.at[group, here], p1_recv.at[group])
        own_lifts(group, lambda copy: copy.start())
        move_inputs(group)
        own_lifts(group + 2, lambda copy: copy.start())
        move_inputs(group + 2)

    @pl.loop(0, 2)
    def _(parity):
        target_level = host_of(parity)

        @pl.loop(0, SEGS)
        def _(column):
            current = column
            for offset in range(1, LEVELS):
                current = parents[jnp.maximum(target_level - offset, 0), 0, current]
                anc[parity, offset, column] = current

        @pl.loop(1, 2 * half(target_level) + 2)
        def _(offset):
            lane = lax.broadcasted_iota(jnp.int32, (PIECE, SEGS * PIECE), 1)
            row = lax.broadcasted_iota(jnp.int32, (PIECE, SEGS * PIECE), 0)
            target = lane % PIECE
            lane_column = lane // PIECE
            for column in range(SEGS):
                found = anc[parity, offset, column] * PIECE
                pick[parity, offset, rows_of(column, PIECE), :] = jnp.where(
                    lane == found + row, 1.0, 0.0
                ).astype(BF16)
                target = target + jnp.where(lane_column == column, found, 0)
            for column in range(SEGS):
                spread[parity, offset, rows_of(column, PIECE), :] = jnp.where(
                    target == row + column * PIECE, 1.0, 0.0
                ).astype(BF16)

    @pl.loop(0, KV_HEADS)
    def _(head):
        @pl.when(host_of(head) == 0)
        def _():
            blocks[head, 1] = jnp.zeros((2, ROWS, HEAD_DIM), BF16)

    def pass_on(head):
        def forward(which, copy):
            wait_bytes(unit(head, which), up_recv.at[head, which])
            copy.start()

        passed_on(head, forward)

    def select(head):
        here = host_of(head)
        parity = odd(head)

        @pl.loop(0, 4)
        def _(plane):
            other = 2 * plane + 1 - core

            @pl.when(other < here)
            def _():
                wait_bytes(unit(head, other), up_recv.at[head, other])

        def send(count):
            for offset in range(1, count + 1):
                found = jnp.dot(
                    pick[parity, offset],
                    pieces[
                        parity, jnp.maximum(here - offset, 0), :, :, lanes(half(head))
                    ].reshape(SEGS * PIECE, HEAD_DIM),
                    preferred_element_type=F32,
                )
                chosen[head, :, offset - 1] = found.astype(BF16).reshape(SEGS, PIECE, HEAD_DIM)
            part, span = piece_of(me)

            @pl.loop(1, SEGS)
            def _(step):
                peer = wrapped(me + step)
                remote(
                    chosen.at[head, peer, pl.ds(0, count)],
                    blocks.at[head, pl.ds(1, count), part, span, :],
                    p3_send.at[head], p3_recv.at[head], (level, peer),
                ).start()

            pltpu.make_async_copy(
                chosen.at[head, me, pl.ds(0, count)],
                blocks.at[head, pl.ds(1, count), part, span, :], p3_recv.at[head],
            ).start()

        per_plane(here, send)

    def attend(head):
        here = host_of(head)
        pairs = half(here) + 1
        contract_last = (((1,), (1,)), ((), ()))
        span_all = [pl.ds(group * ROWS, ROWS) for group in range(GROUP)]

        def block_pair(pair, part):
            return blocks[head, pl.ds(2 * pair, 2), part].reshape(PAIR, HEAD_DIM)

        stats[0] = jnp.full((8, STACK), NEG_FILL, F32)
        for index in range(2):
            for group, span in enumerate(span_all):
                stacks[index, span, :] = inputs[head, index, :, span]

        @pl.loop(0, pairs)
        def _(pair):
            span_rows = rows_of(pair, PAIR)
            logits[span_rows, :] = lax.dot_general(
                block_pair(pair, 0), stacks[0], contract_last, preferred_element_type=F32
            )
            grad_probs[span_rows, :] = lax.dot_general(
                block_pair(pair, 1), stacks[1], contract_last, preferred_element_type=F32
            )

            @pl.when(pair == 0)
            def _():
                u_row = lax.broadcasted_iota(jnp.int32, (ROWS, ROWS), 0)
                t_row = lax.broadcasted_iota(jnp.int32, (ROWS, ROWS), 1)
                for span in span_all:
                    logits[0:ROWS, span] = jnp.where(
                        u_row <= t_row, logits[0:ROWS, span], NEG_FILL
                    )

            @pl.when((pair == pairs - 1) & (odd(here) == 0))
            def _():
                logits[rows_of(here + 1, ROWS), :] = jnp.full((ROWS, STACK), NEG_FILL, F32)

            for span in span_all:
                stats[0, :, span] = jnp.maximum(
                    stats[0, :, span], fold(logits[span_rows, span]).max(0)
                )

        stats[1] = jnp.zeros((8, STACK), F32)
        stats[2] = jnp.zeros((8, STACK), F32)
        stats[0] = jnp.broadcast_to(stats[0].max(0, keepdims=True), (8, STACK))

        @pl.loop(0, pairs)
        def _(pair):
            span_rows = rows_of(pair, PAIR)
            for span in span_all:
                top = stats[0, 0:1, span]
                tile = jnp.exp2((logits[span_rows, span] - top) * EXP2_SCALE)
                logits[span_rows, span] = tile
                stats[1, :, span] += fold(tile).sum(0)
                stats[2, :, span] += fold(tile * grad_probs[span_rows, span]).sum(0)

        inverse = 1.0 / stats[1].sum(0, keepdims=True)
        delta = stats[2].sum(0, keepdims=True) * inverse
        stats[1] = jnp.broadcast_to(inverse, (8, STACK))
        stats[2] = jnp.broadcast_to(delta, (8, STACK))
        query_sum[...] = jnp.zeros((HEAD_DIM, STACK), F32)

        @pl.loop(0, pairs)
        def _(pair):
            span_rows = rows_of(pair, PAIR)
            for span in span_all:
                exact = logits[span_rows, span] * stats[1, 0:1, span]
                probs[:, span] = exact.astype(BF16)
                grad_logits[:, span] = (
                    exact * (grad_probs[span_rows, span] - stats[2, 0:1, span])
                ).astype(BF16)
            value_term = jnp.dot(probs[...], stacks[1], preferred_element_type=F32)
            key_term = SCALE * jnp.dot(
                grad_logits[...], stacks[0], preferred_element_type=F32
            )
            for part, term in enumerate((key_term, value_term)):
                terms[head, pl.ds(2 * pair, 2), part] = term.astype(BF16).reshape(
                    2, ROWS, HEAD_DIM
                )

                @pl.when(pair == 0)
                def _():
                    own[head, part] = term[0:ROWS]

            query_sum[...] += lax.dot_general(
                block_pair(pair, 0), grad_logits[...], (((0,), (0,)), ((), ())),
                preferred_element_type=F32,
            )

        for group, span in enumerate(span_all):
            staged[head, :, span] = (SCALE * query_sum[:, span].T).astype(BF16)

    def query_target(head):
        return grad_queries.at[0, 0, :, lanes(name_of(head), GROUP)]

    def send_results(head):
        host = host_of(head)
        here = host

        def send(count):
            @pl.loop(1, SEGS)
            def _(step):
                peer = wrapped(me + step)
                part, span = piece_of(peer)
                remote(
                    terms.at[head, pl.ds(1, count), part, span, :],
                    term_pieces.at[head, pl.ds(1, count), me],
                    b1_send.at[head], b1_recv.at[head], (level, peer),
                ).start()

            part, span = piece_of(me)
            pltpu.make_async_copy(
                terms.at[head, pl.ds(1, count), part, span, :],
                term_pieces.at[head, pl.ds(1, count), me], b1_recv.at[head],
            ).start()

        per_plane(here, send)
        move(
            head, staged.at[head], query_target(head), d_send.at[head], d_recv.at[head]
        )

        @pl.when(host != level)
        def _():
            own_out[head] = own[head].astype(BF16)
            remote(
                own_out.at[head], own_in.at[head], o_send.at[head], o_recv.at[head], (host, me)
            ).start()

    def summed(head, offset):
        return jnp.dot(
            spread[odd(head), offset],
            term_pieces[head, offset].reshape(SEGS * PIECE, HEAD_DIM),
            preferred_element_type=F32,
        )

    def cross_copy(head, plane):
        return remote(
            cross_out.at[head, plane], cross_in.at[head, plane],
            x_send.at[head, plane], x_recv.at[head, plane], (sibling, me),
        )

    def sum_stage(head):
        here = host_of(head)

        def sums(count):
            wait_bytes(term_pieces.at[head, pl.ds(1, count)], b1_recv.at[head])
            for plane in range((count + 1) // 2):
                offset = jnp.maximum(here - (2 * plane + 1 - core), 1)
                cross_out[head, plane] = summed(head, offset).astype(BF16)
            for plane in range((count - 1) // 2):
                offset = jnp.maximum(here - (2 * plane + core), 1)
                kept[head, plane] = summed(head, offset)

        per_plane(here, sums)

        @pl.loop(0, 4)
        def _(plane):
            @pl.when(here - (2 * plane + 1 - core) >= 1)
            def _():
                cross_copy(head, plane).start()

    def climb_copy(head, plane):
        slot = half(host_of(head)) - 1
        return remote(
            climb_out.at[head, plane], climb_in.at[head, slot],
            c_send.at[head, plane], c_recv.at[head, slot], (device_of(head, plane), me),
        )

    def climb(head):
        plane_here = half(host_of(head))

        @pl.loop(0, plane_here - core + 1)
        def _(plane):
            wait_bytes(cross_in.at[head, plane], x_recv.at[head, plane])

        @pl.loop(0, plane_here)
        def _(plane):
            climb_out[head, plane] = (
                kept[head, plane] + cross_in[head, plane].astype(F32)
            ).astype(BF16)
            climb_copy(head, plane).start()

    def final_send(head):
        host = host_of(head)

        @pl.when(host < LEVELS - 1)
        def _():
            total_sum[...] = jnp.zeros((SEGS * PIECE, HEAD_DIM), F32)

            @pl.loop(half(host), 3)
            def _(slot):
                wait_bytes(climb_in.at[head, slot], c_recv.at[head, slot])
                total_sum[...] += climb_in[head, slot].astype(F32)

            @pl.when(core == 0)
            def _():
                total_sum[...] += cross_in[head, half(host)].astype(F32)

            final_out[head] = total_sum[...].astype(BF16).reshape(SEGS, PIECE, HEAD_DIM)
            part, span = piece_of(me)

            @pl.loop(1, SEGS)
            def _(step):
                peer = wrapped(me + step)
                remote(
                    final_out.at[head, peer], final_in.at[head, part, span, :],
                    f_send.at[head], f_recv.at[head], (host, peer),
                ).start()

            move(
                head, final_out.at[head, me], final_in.at[head, part, span, :],
                f_send.at[head], f_recv.at[head],
            )

    def final_store(head):
        away = host_of(head) != level

        @pl.when(away)
        def _():
            wait_bytes(own_in.at[head], o_recv.at[head])
            own[head] = own_in[head].astype(F32)

        @pl.when(level < LEVELS - 1)
        def _():
            wait_bytes(final_in.at[head], f_recv.at[head])
            own[head] = own[head] + final_in[head].astype(F32)

        grad_kv[0, 0, :, :, lanes(name_of(head))] = own[head].astype(BF16)

    stages = (sum_stage, climb, final_send, final_store)

    @pl.loop(0, KV_HEADS + LAG + len(stages))
    def _(tick):
        @pl.when(tick < KV_HEADS)
        def _():
            pass_on(tick)

        @pl.when((tick >= 1) & (tick < KV_HEADS + 1))
        def _():
            select(tick - 1)

        @pl.when((tick >= LAG) & (tick < KV_HEADS + LAG))
        def _():
            head = tick - LAG
            per_plane(
                host_of(head),
                lambda count: wait_bytes(blocks.at[head, pl.ds(1, count)], p3_recv.at[head]),
            )
            wait_bytes(blocks.at[head, 0], k_recv.at[head])
            wait_bytes(inputs.at[head], q_recv.at[head])
            attend(head)
            send_results(head)

        for lag, stage in enumerate(stages, LAG + 1):
            @pl.when((tick >= lag) & (tick < KV_HEADS + lag))
            def _():
                stage(tick - lag)

    @pl.loop(0, 2)
    def _(group):
        wait_bytes(pieces.at[group, 0, pl.ds(1, SEGS - 1)], p1_send.at[group])

        @pl.when(host_of(group) != level)
        def _():
            wait_bytes(pieces.at[group, 0, 0], p1_send.at[group])

    @pl.loop(0, KV_HEADS)
    def _(head):
        host = host_of(head)
        away = host != level
        wait_bytes(query_target(head), d_recv.at[head])
        own_lifts(head, lambda copy: copy.wait_send())
        passed_on(head, lambda which, copy: copy.wait_send())

        @pl.when(away)
        def _():
            wait_bytes(blocks.at[head, 0], k_send.at[head])
            wait_bytes(inputs.at[head], q_send.at[head])
            wait_bytes(staged.at[head], d_send.at[head])
            wait_bytes(own_out.at[head], o_send.at[head])

        def sent(count):
            wait_bytes(chosen.at[head, pl.ds(1, SEGS - 1), pl.ds(0, count)], p3_send.at[head])
            wait_bytes(
                term_pieces.at[head, pl.ds(1, count), pl.ds(1, SEGS - 1)], b1_send.at[head]
            )

        per_plane(host, sent)

        @pl.loop(0, 4)
        def _(plane):
            @pl.when(host - (2 * plane + 1 - core) >= 1)
            def _():
                cross_copy(head, plane).wait_send()

        @pl.loop(0, half(host))
        def _(plane):
            climb_copy(head, plane).wait_send()

        @pl.when(host < LEVELS - 1)
        def _():
            wait_bytes(final_out.at[head, pl.ds(1, SEGS - 1)], f_send.at[head])

            @pl.when(away)
            def _():
                wait_bytes(final_out.at[head, 0], f_send.at[head])


def shards(queries, keys_values, grad_out, parents):
    vmem = pl.BlockSpec(memory_space=pltpu.VMEM)
    smem = pl.BlockSpec(memory_space=pltpu.SMEM)
    anywhere = pl.BlockSpec(memory_space=pl.ANY)
    dma = pltpu.SemaphoreType.DMA
    tile = (SEGS, PIECE, HEAD_DIM)
    flat = (SEGS * PIECE, HEAD_DIM)
    keys_count = LEVELS * ROWS
    part_pair = (2, ROWS, HEAD_DIM)
    selectors = (2, LEVELS, SEGS * PIECE, SEGS * PIECE)
    scratch = [
        pltpu.SMEM((2, LEVELS, SEGS), jnp.int32),
        pltpu.VMEM(selectors, BF16),
        pltpu.VMEM(selectors, BF16),
        pltpu.VMEM((2, LEVELS, SEGS, PIECE, 2 * HEAD_DIM), BF16),
        pltpu.VMEM((KV_HEADS, SEGS, LEVELS - 1, PIECE, HEAD_DIM), BF16),
        pltpu.VMEM((KV_HEADS, LEVELS) + part_pair, BF16),
        pltpu.VMEM((KV_HEADS, LEVELS) + part_pair, BF16),
        pltpu.VMEM((KV_HEADS, LEVELS) + tile, BF16),
        pltpu.VMEM((KV_HEADS,) + part_pair, F32),
        pltpu.VMEM((KV_HEADS,) + part_pair, BF16),
        pltpu.VMEM((KV_HEADS,) + part_pair, BF16),
        pltpu.VMEM((KV_HEADS, 2, ROWS, STACK), BF16),
        pltpu.VMEM((2, STACK, HEAD_DIM), BF16),
        pltpu.VMEM((KV_HEADS, ROWS, STACK), BF16),
        pltpu.VMEM((HEAD_DIM, STACK), F32),
        pltpu.VMEM((3, 8, STACK), F32),
        pltpu.VMEM((keys_count, STACK), F32),
        pltpu.VMEM((keys_count, STACK), F32),
        pltpu.VMEM((PAIR, STACK), BF16),
        pltpu.VMEM((PAIR, STACK), BF16),
        pltpu.VMEM((KV_HEADS, 3) + flat, F32),
        pltpu.VMEM(flat, F32),
        pltpu.VMEM((KV_HEADS, 4) + flat, BF16),
        pltpu.VMEM((KV_HEADS, 4) + flat, BF16),
        pltpu.VMEM((KV_HEADS, 3) + flat, BF16),
        pltpu.VMEM((KV_HEADS, 3) + flat, BF16),
        pltpu.VMEM((KV_HEADS,) + tile, BF16),
        pltpu.VMEM((KV_HEADS,) + part_pair, BF16),
        dma((2,)), dma((2,)),
        dma((KV_HEADS, 7)), dma((KV_HEADS, LEVELS)),
        dma((KV_HEADS,)), dma((KV_HEADS,)),
        dma((KV_HEADS,)), dma((KV_HEADS,)),
        dma((KV_HEADS,)), dma((KV_HEADS,)),
        dma((KV_HEADS,)), dma((KV_HEADS,)),
        dma((KV_HEADS,)), dma((KV_HEADS,)),
        dma((KV_HEADS,)), dma((KV_HEADS,)),
        dma((KV_HEADS, 4)), dma((KV_HEADS, 4)),
        dma((KV_HEADS, 3)), dma((KV_HEADS, 3)),
        dma((KV_HEADS,)), dma((KV_HEADS,)),
    ]
    return pl.pallas_call(
        kernel,
        out_shape=(
            jax.ShapeDtypeStruct(queries.shape, BF16),
            jax.ShapeDtypeStruct(keys_values.shape, BF16),
        ),
        in_specs=[smem, anywhere, anywhere, anywhere],
        out_specs=(vmem, vmem),
        scratch_shapes=scratch,
        compiler_params=pltpu.CompilerParams(
            collective_id=0, has_side_effects=True, vmem_limit_bytes=56 * 1024 * 1024
        ),
        cost_estimate=pl.CostEstimate(
            flops=5 * 2 * HEADS * LEVELS * ROWS * ROWS * HEAD_DIM,
            bytes_accessed=8 * 1024 * 1024,
            transcendentals=HEADS * LEVELS * ROWS * ROWS,
        ),
    )(parents.transpose(0, 2, 1), queries, keys_values, grad_out)


def solution(mesh):
    in_specs = (
        P("depth", "seg", None, None),
        P("depth", "seg", None, None, None),
        P("depth", "seg", None, None),
        P(),
    )
    out_specs = (P("depth", "seg", None, None), P("depth", "seg", None, None, None))
    return jax.shard_map(shards, mesh=mesh, in_specs=in_specs, out_specs=out_specs, check_vma=False)
```

time: 83.3 us -> 82.5 us (level)
  no operation moved by 1% of the time
where the time goes in v1:
time: 82.5 us; the launch traced here: 82.1 us
  Pallas kernels  78.8 us (96%)
  local copies, waits for them, and re-layouts  2.71 us (3%)
    pallas_call x1, Pallas kernels, shards(): pl.pallas_call(kernel, out_shape=(jax.ShapeDtypeStruct(queries.shape, BF1...  78.8 us
    unnamed x4, local copies, waits for them, and re-layouts  2.71 us

profile of v1, /device:TPU:0, one launch (start us, length us, event | category | flops | bytes accessed | tf_op | source)
XLA Modules:
  0.0 82.1 jit_solution(4263957757767224652)
XLA Ops:
  0.6 78.8 %shard_map.59 = (bf16[1,1,128,2560]{3,2,1,0:T(8,128)(2,1)}, bf16[1,1,2,128,512]{4,3,2,1,0:T(8,128)(2,1)}) custom-call(s32[7,1,16]{2,1,0:T(1,128)} %bitcast.1, bf16[1,1,128,2560]{3,2,1,0:T(8,128)(2,1)} %queries.1, bf16[1,1,2,128,512]{4,3,2,1,0:T(8,128)(2,1)} %keys_values.1, bf16[1,1,128,2560]{3,2,1,0:T(8,128)(2,1)} %grad_out.1), custom_call_target="tpu_custom_call" | custom-call | flops 3355443200 | bytes 8388608 | tf_op jit(solution)/shard_map/pallas_call | solution.py:651
  79.4 0.0 copy-start
  79.4 2.0 %copy.8 = bf16[1,1,128,2560]{3,2,1,0:T(8,128)(2,1)} copy(bf16[1,1,128,2560]{3,2,1,0:T(8,128)(2,1)} %get-tuple-element.4) | data formatting | bytes 1310720
  81.4 0.0 copy-done
  81.4 0.7 copy.9
Async XLA Ops:
  79.4 2.0 %copy-start = (bf16[1,1,2,128,512]{4,3,2,1,0:T(8,128)(2,1)S(1)}, bf16[1,1,2,128,512]{4,3,2,1,0:T(8,128)(2,1)}, u32[]{:S(2)}) copy-start(bf16[1,1,2,128,512]{4,3,2,1,0:T(8,128)(2,1)} %get-tuple-element.5) | copy-start | bytes 786436

commit v2 on v1

--- a/solution.py
+++ b/solution.py
@@ -19,6 +19,7 @@
 STACK = GROUP * ROWS
 PAIR = 2 * ROWS
 LAG = 2
+SWAPPED = 1
 
 NEG_FILL = -1e30
 SCALE = HEAD_DIM ** -0.5
@@ -36,8 +37,16 @@
     return lax.rem(value, 2)
 
 
+def is_swapped(head):
+    return head == SWAPPED
+
+
 def name_of(head):
-    return 2 * odd(head) + half(head)
+    return jnp.where(is_swapped(head), KV_HEADS - 1, head - jnp.where(head > SWAPPED, 1, 0))
+
+
+def group_of(head):
+    return jnp.where(is_swapped(head), 1, 0)
 
 
 def wrapped(index):
@@ -65,7 +74,7 @@
 def kernel(
     parents, queries, keys_values, grad_out, grad_queries, grad_kv,
     anc, pick, spread, pieces, chosen, blocks, terms, term_pieces, own, own_out, own_in,
-    inputs, stacks, staged, query_sum, stats, logits, grad_probs, probs, grad_logits,
+    inputs, stacks, turned, staged, query_sum, stats, logits, grad_probs, probs, grad_logits,
     kept, total_sum, cross_out, cross_in, climb_out, climb_in, final_out, final_in,
     p1_send, p1_recv, up_send, up_recv, q_send, q_recv, k_send, k_recv, p3_send, p3_recv,
     b1_send, b1_recv, o_send, o_recv, d_send, d_recv, x_send, x_recv, c_send, c_recv,
@@ -80,10 +89,10 @@
     partner = jnp.where(outer, 2 * (3 - y) + core, level)
 
     def host_of(head):
-        return jnp.where(odd(head) == 1, partner, level)
+        return jnp.where(is_swapped(head), partner, level)
 
     def device_of(head, plane):
-        swapped = (odd(head) == 1) & ((plane == 0) | (plane == 3))
+        swapped = is_swapped(head) & ((plane == 0) | (plane == 3))
         return 2 * jnp.where(swapped, 3 - plane, plane) + core
 
     def remote(src, dst, send_sem, recv_sem, device):
@@ -112,6 +121,12 @@
         def _():
             pltpu.make_async_copy(src, dst, recv_sem).start()
 
+    kept_width = (KV_HEADS - 1) * HEAD_DIM
+    spread_groups = (
+        (level, pl.ds(0, kept_width)),
+        (partner, pl.ds(kept_width, HEAD_DIM)),
+    )
+
     barrier = pltpu.get_barrier_semaphore()
 
     def greet(device):
@@ -133,34 +148,31 @@
 
     pl.semaphore_wait(barrier, SEGS - 1 + 4 + jnp.where(outer, SEGS, 0))
 
-    @pl.loop(0, 2)
-    def _(group):
-        host = host_of(group)
-
+    for group, (host, span_lanes) in enumerate(spread_groups):
         def source(peer):
             part, span = piece_of(peer)
-            return keys_values.at[0, 0, part, span, lanes(group, 2)]
+            return keys_values.at[0, 0, part, span, span_lanes]
+
+        def landing():
+            return pieces.at[level, me, :, span_lanes]
 
         @pl.loop(1, SEGS)
         def _(step):
             peer = wrapped(me + step)
             remote(
-                source(peer), pieces.at[group, level, me],
-                p1_send.at[group], p1_recv.at[group], (host, peer),
+                source(peer), landing(), p1_send.at[group], p1_recv.at[group], (host, peer)
             ).start()
 
-        @pl.when(host != level)
-        def _():
-            remote(
-                source(me), pieces.at[group, level, me],
-                p1_send.at[group], p1_recv.at[group], (host, me),
-            ).start()
+        if group == 1:
+            @pl.when(host != level)
+            def _():
+                remote(
+                    source(me), landing(), p1_send.at[group], p1_recv.at[group], (host, me)
+                ).start()
 
         @pl.when(host == level)
         def _():
-            pltpu.make_async_copy(
-                source(me), pieces.at[group, level, me], p1_recv.at[group]
-            ).start()
+            pltpu.make_async_copy(source(me), landing(), p1_recv.at[group]).start()
 
     def move_inputs(head):
         name = name_of(head)
@@ -175,7 +187,7 @@
             )
 
     def unit(head, which):
-        return pieces.at[odd(head), which, :, :, lanes(half(head))]
+        return pieces.at[which, :, :, lanes(name_of(head))]
 
     def lift(head, which, slot, device):
         return remote(
@@ -200,17 +212,20 @@
         def _(plane):
             action(2 * plane + core, lift(head, 2 * plane + core, 4 + plane, sibling))
 
-    for group in range(2):
-        here = host_of(group)
-        wait_bytes(pieces.at[group, here], p1_recv.at[group])
-        own_lifts(group, lambda copy: copy.start())
-        move_inputs(group)
-        own_lifts(group + 2, lambda copy: copy.start())
-        move_inputs(group + 2)
+    for group, (host, span_lanes) in enumerate(spread_groups):
+        wait_bytes(pieces.at[host, :, :, span_lanes], p1_recv.at[group])
+
+    @pl.loop(0, KV_HEADS)
+    def _(head):
+        own_lifts(head, lambda copy: copy.start())
+
+    @pl.loop(0, KV_HEADS)
+    def _(head):
+        move_inputs(head)
 
     @pl.loop(0, 2)
     def _(parity):
-        target_level = host_of(parity)
+        target_level = jnp.where(parity == 1, partner, level)
 
         @pl.loop(0, SEGS)
         def _(column):
@@ -223,8 +238,8 @@
         def _(offset):
             lane = lax.broadcasted_iota(jnp.int32, (PIECE, SEGS * PIECE), 1)
             row = lax.broadcasted_iota(jnp.int32, (PIECE, SEGS * PIECE), 0)
-            target = lane % PIECE
-            lane_column = lane // PIECE
+            target = lane & (PIECE - 1)
+            lane_column = lane >> 4
             for column in range(SEGS):
                 found = anc[parity, offset, column] * PIECE
                 pick[parity, offset, rows_of(column, PIECE), :] = jnp.where(
@@ -251,7 +266,7 @@
 
     def select(head):
         here = host_of(head)
-        parity = odd(head)
+        parity = group_of(head)
 
         @pl.loop(0, 4)
         def _(plane):
@@ -266,7 +281,7 @@
                 found = jnp.dot(
                     pick[parity, offset],
                     pieces[
-                        parity, jnp.maximum(here - offset, 0), :, :, lanes(half(head))
+                        jnp.maximum(here - offset, 0), :, :, lanes(name_of(head))
                     ].reshape(SEGS * PIECE, HEAD_DIM),
                     preferred_element_type=F32,
                 )
@@ -292,7 +307,6 @@
     def attend(head):
         here = host_of(head)
         pairs = half(here) + 1
-        contract_last = (((1,), (1,)), ((), ()))
         span_all = [pl.ds(group * ROWS, ROWS) for group in range(GROUP)]
 
         def block_pair(pair, part):
@@ -301,16 +315,18 @@
         stats[0] = jnp.full((8, STACK), NEG_FILL, F32)
         for index in range(2):
             for group, span in enumerate(span_all):
-                stacks[index, span, :] = inputs[head, index, :, span]
+                tile = inputs[head, index, :, span]
+                stacks[index, span, :] = tile
+                turned[index, :, span] = tile.T
 
         @pl.loop(0, pairs)
         def _(pair):
             span_rows = rows_of(pair, PAIR)
-            logits[span_rows, :] = lax.dot_general(
-                block_pair(pair, 0), stacks[0], contract_last, preferred_element_type=F32
-            )
-            grad_probs[span_rows, :] = lax.dot_general(
-                block_pair(pair, 1), stacks[1], contract_last, preferred_element_type=F32
+            logits[span_rows, :] = jnp.dot(
+                block_pair(pair, 0), turned[0], preferred_element_type=F32
+            )
+            grad_probs[span_rows, :] = jnp.dot(
+                block_pair(pair, 1), turned[1], preferred_element_type=F32
             )
 
             @pl.when(pair == 0)
@@ -419,7 +435,7 @@
 
     def summed(head, offset):
         return jnp.dot(
-            spread[odd(head), offset],
+            spread[group_of(head), offset],
             term_pieces[head, offset].reshape(SEGS * PIECE, HEAD_DIM),
             preferred_element_type=F32,
         )
@@ -547,13 +563,12 @@
             def _():
                 stage(tick - lag)
 
-    @pl.loop(0, 2)
-    def _(group):
-        wait_bytes(pieces.at[group, 0, pl.ds(1, SEGS - 1)], p1_send.at[group])
-
-        @pl.when(host_of(group) != level)
-        def _():
-            wait_bytes(pieces.at[group, 0, 0], p1_send.at[group])
+    for group, (host, span_lanes) in enumerate(spread_groups):
+        wait_bytes(pieces.at[0, pl.ds(1, SEGS - 1), :, span_lanes], p1_send.at[group])
+        if group == 1:
+            @pl.when(host != level)
+            def _():
+                wait_bytes(pieces.at[0, 0, :, span_lanes], p1_send.at[group])
 
     @pl.loop(0, KV_HEADS)
     def _(head):
@@ -611,7 +626,7 @@
         pltpu.SMEM((2, LEVELS, SEGS), jnp.int32),
         pltpu.VMEM(selectors, BF16),
         pltpu.VMEM(selectors, BF16),
-        pltpu.VMEM((2, LEVELS, SEGS, PIECE, 2 * HEAD_DIM), BF16),
+        pltpu.VMEM((LEVELS, SEGS, PIECE, KV_HEADS * HEAD_DIM), BF16),
         pltpu.VMEM((KV_HEADS, SEGS, LEVELS - 1, PIECE, HEAD_DIM), BF16),
         pltpu.VMEM((KV_HEADS, LEVELS) + part_pair, BF16),
         pltpu.VMEM((KV_HEADS, LEVELS) + part_pair, BF16),
@@ -621,6 +636,7 @@
         pltpu.VMEM((KV_HEADS,) + part_pair, BF16),
         pltpu.VMEM((KV_HEADS, 2, ROWS, STACK), BF16),
         pltpu.VMEM((2, STACK, HEAD_DIM), BF16),
+        pltpu.VMEM((2, HEAD_DIM, STACK), BF16),
         pltpu.VMEM((KV_HEADS, ROWS, STACK), BF16),
         pltpu.VMEM((HEAD_DIM, STACK), F32),
         pltpu.VMEM((3, 8, STACK), F32),

time: 82.5 us -> 87.7 us (1.063)
  Pallas kernels: 78.8 us -> 84 us
    pallas_call x1, Pallas kernels: 78.8 us -> 84 us  [shards(): pl.pallas_call(kernel, out_shape=(jax.ShapeDtypeStruct(queries.shape, BF1...]
where the time goes in v2:
time: 87.7 us; the launch traced here: 87.4 us
  Pallas kernels  84 us (96%)
  local copies, waits for them, and re-layouts  2.71 us (3%)
    pallas_call x1, Pallas kernels, shards(): pl.pallas_call(kernel, out_shape=(jax.ShapeDtypeStruct(queries.shape, BF1...  84 us
    unnamed x4, local copies, waits for them, and re-layouts  2.71 us

profile of v2, /device:TPU:0, one launch (start us, length us, event | category | flops | bytes accessed | tf_op | source)
XLA Modules:
  0.0 87.4 jit_solution(2631069327577746135)
XLA Ops:
  0.6 84.0 %shard_map.59 = (bf16[1,1,128,2560]{3,2,1,0:T(8,128)(2,1)}, bf16[1,1,2,128,512]{4,3,2,1,0:T(8,128)(2,1)}) custom-call(s32[7,1,16]{2,1,0:T(1,128)} %bitcast.1, bf16[1,1,128,2560]{3,2,1,0:T(8,128)(2,1)} %queries.1, bf16[1,1,2,128,512]{4,3,2,1,0:T(8,128)(2,1)} %keys_values.1, bf16[1,1,128,2560]{3,2,1,0:T(8,128)(2,1)} %grad_out.1), custom_call_target="tpu_custom_call" | custom-call | flops 3355443200 | bytes 8388608 | tf_op jit(solution)/shard_map/pallas_call | solution.py:667
  84.7 0.0 copy-start
  84.7 2.0 %copy.8 = bf16[1,1,128,2560]{3,2,1,0:T(8,128)(2,1)} copy(bf16[1,1,128,2560]{3,2,1,0:T(8,128)(2,1)} %get-tuple-element.4) | data formatting | bytes 1310720
  86.7 0.0 copy-done
  86.7 0.7 copy.9
Async XLA Ops:
  84.7 2.0 %copy-start = (bf16[1,1,2,128,512]{4,3,2,1,0:T(8,128)(2,1)S(1)}, bf16[1,1,2,128,512]{4,3,2,1,0:T(8,128)(2,1)}, u32[]{:S(2)}) copy-start(bf16[1,1,2,128,512]{4,3,2,1,0:T(8,128)(2,1)} %get-tuple-element.5) | copy-start | bytes 786436

commit v3 on v2

v3 whole, which is shorter than its diff:
```python
import functools

import jax
import jax.numpy as jnp
from jax import lax
from jax.experimental import pallas as pl
from jax.experimental.pallas import tpu as pltpu
from jax.sharding import PartitionSpec as P

HEADS = 20
KV_HEADS = 4
HEAD_DIM = 128
GROUP = HEADS // KV_HEADS
ROWS = 128
LEVELS = 8
SEGS = 16
PIECE = 16
PIECES_PER_PART = ROWS // PIECE
STACK = GROUP * ROWS
PAIR = 2 * ROWS

NEG_FILL = -1e30
SCALE = HEAD_DIM ** -0.5
EXP2_SCALE = SCALE * 1.4426950408889634
MESH = pl.DeviceIdType.MESH
BF16 = jnp.bfloat16
F32 = jnp.float32


def half(value):
    return lax.div(value, 2)


def odd(value):
    return lax.rem(value, 2)


def wrapped(index):
    return jnp.where(index >= SEGS, index - SEGS, index)


def lanes(index, count=1):
    width = count * HEAD_DIM
    return pl.ds(pl.multiple_of(index * width, width), width)


def rows_of(index, count):
    return pl.ds(pl.multiple_of(index * count, count), count)


def piece_of(index):
    part = jnp.where(index >= PIECES_PER_PART, 1, 0)
    return part, rows_of(index - part * PIECES_PER_PART, PIECE)


def fold(tile):
    return tile.reshape(tile.shape[0] // 8, 8, tile.shape[1])


def place():
    level = lax.axis_index("depth")
    return level, lax.axis_index("seg"), half(level), odd(level)


def host_of(head):
    return lax.axis_index("depth")


def device_of(head, plane):
    return 2 * plane + odd(lax.axis_index("depth"))


def remote(src, dst, send_sem, recv_sem, device):
    return pltpu.make_async_remote_copy(
        src_ref=src, dst_ref=dst, send_sem=send_sem, recv_sem=recv_sem,
        device_id=device, device_id_type=MESH,
    )


def wait_bytes(ref, sem):
    pltpu.make_async_copy(ref, ref, sem).wait()


def per_plane(which, action):
    for plane in range(LEVELS // 2):
        pl.when((which > 0) & (half(which) == plane))(
            functools.partial(action, 2 * plane + 1)
        )


def enter():
    level, me, y, core = place()
    barrier = pltpu.get_barrier_semaphore()

    def greet(device):
        pl.semaphore_signal(barrier, inc=1, device_id=device, device_id_type=MESH)

    @pl.loop(1, SEGS)
    def _(step):
        greet((level, wrapped(me + step)))

    greet((2 * y + 1 - core, me))
    for step in range(1, 4):
        greet((lax.rem(level + 2 * step, LEVELS), me))
    pl.semaphore_wait(barrier, SEGS - 1 + 4)


def find_ancestors(parents, anc, level):
    @pl.loop(0, SEGS)
    def _(column):
        current = column
        for offset in range(1, LEVELS):
            current = parents[jnp.maximum(level - offset, 0), 0, current]
            anc[offset, column] = current


def make_pick(pick, anc, level):
    @pl.loop(1, 2 * half(level) + 2)
    def _(offset):
        lane = lax.broadcasted_iota(jnp.int32, (PIECE, SEGS * PIECE), 1)
        row = lax.broadcasted_iota(jnp.int32, (PIECE, SEGS * PIECE), 0)
        for column in range(SEGS):
            pick[offset, rows_of(column, PIECE), :] = jnp.where(
                lane == anc[offset, column] * PIECE + row, 1.0, 0.0
            ).astype(BF16)


def make_spread(spread, anc, level):
    @pl.loop(1, 2 * half(level) + 2)
    def _(offset):
        lane = lax.broadcasted_iota(jnp.int32, (PIECE, SEGS * PIECE), 1)
        row = lax.broadcasted_iota(jnp.int32, (PIECE, SEGS * PIECE), 0)
        target = lane & (PIECE - 1)
        lane_column = lane >> 4
        for column in range(SEGS):
            target = target + jnp.where(lane_column == column, anc[offset, column] * PIECE, 0)
        for column in range(SEGS):
            spread[offset, rows_of(column, PIECE), :] = jnp.where(
                target == row + column * PIECE, 1.0, 0.0
            ).astype(BF16)


def gather_kernel(
    parents, keys_values, blocks,
    anc, pick, pieces, chosen,
    p1_send, p1_recv, up_send, up_recv, p3_send, p3_recv,
):
    level, me, y, core = place()
    sibling = 2 * y + 1 - core
    enter()

    def source(peer):
        part, span = piece_of(peer)
        return keys_values.at[0, 0, part, span, :]

    @pl.loop(1, SEGS)
    def _(step):
        peer = wrapped(me + step)
        remote(source(peer), pieces.at[level, me], p1_send, p1_recv, (level, peer)).start()

    pltpu.make_async_copy(source(me), pieces.at[level, me], p1_recv).start()

    def unit(head, which):
        return pieces.at[which, :, :, lanes(head)]

    def lift(head, which, slot, device):
        return remote(
            unit(head, which), unit(head, which),
            up_send.at[head, slot], up_recv.at[head, which], (device, me),
        )

    def own_lifts(head, action):
        here = host_of(head)
        plane = half(here)
        for step in range(1, 4):
            @pl.when(plane + step <= 3)
            def _():
                action(lift(head, here, step - 1, device_of(head, plane + step)))

        @pl.when(core == 0)
        def _():
            action(lift(head, here, 3, sibling))

    def passed_on(head, action):
        @pl.loop(0, half(host_of(head)))
        def _(plane):
            action(2 * plane + core, lift(head, 2 * plane + core, 4 + plane, sibling))

    find_ancestors(parents, anc, level)
    wait_bytes(pieces.at[level], p1_recv)

    @pl.loop(0, KV_HEADS)
    def _(head):
        own_lifts(head, lambda copy: copy.start())

    make_pick(pick, anc, level)

    @pl.loop(0, KV_HEADS)
    def _(head):
        blocks[head, 0] = keys_values[0, 0, :, :, lanes(head)]

        @pl.when(level == 0)
        def _():
            blocks[head, 1] = jnp.zeros((2, ROWS, HEAD_DIM), BF16)

    def pass_on(head):
        def forward(which, copy):
            wait_bytes(unit(head, which), up_recv.at[head, which])
            copy.start()

        passed_on(head, forward)

    def select(head):
        here = host_of(head)

        @pl.loop(0, 4)
        def _(plane):
            other = 2 * plane + 1 - core

            @pl.when(other < here)
            def _():
                wait_bytes(unit(head, other), up_recv.at[head, other])

        def send(count):
            for offset in range(1, count + 1):
                found = jnp.dot(
                    pick[offset],
                    pieces[
                        jnp.maximum(here - offset, 0), :, :, lanes(head)
                    ].reshape(SEGS * PIECE, HEAD_DIM),
                    preferred_element_type=F32,
                )
                chosen[head, :, offset - 1] = found.astype(BF16).reshape(SEGS, PIECE, HEAD_DIM)
            part, span = piece_of(me)

            @pl.loop(1, SEGS)
            def _(step):
                peer = wrapped(me + step)
                remote(
                    chosen.at[head, peer, pl.ds(0, count)],
                    blocks.at[head, pl.ds(1, count), part, span, :],
                    p3_send.at[head], p3_recv.at[head], (level, peer),
                ).start()

            pltpu.make_async_copy(
                chosen.at[head, me, pl.ds(0, count)],
                blocks.at[head, pl.ds(1, count), part, span, :], p3_recv.at[head],
            ).start()

        per_plane(here, send)

    @pl.loop(0, KV_HEADS)
    def _(head):
        pass_on(head)

    @pl.loop(0, KV_HEADS)
    def _(head):
        select(head)

    wait_bytes(pieces.at[0, pl.ds(1, SEGS - 1)], p1_send)

    @pl.loop(0, KV_HEADS)
    def _(head):
        own_lifts(head, lambda copy: copy.wait_send())
        passed_on(head, lambda which, copy: copy.wait_send())

        def settle(count):
            wait_bytes(blocks.at[head, pl.ds(1, count)], p3_recv.at[head])
            wait_bytes(chosen.at[head, pl.ds(1, SEGS - 1), pl.ds(0, count)], p3_send.at[head])

        per_plane(level, settle)


def attend_kernel(
    blocks, queries, grad_out, grad_queries, terms, own,
    stacks, turned, query_sum, stats, logits, grad_probs, probs, grad_logits,
):
    def attend(head):
        here = host_of(head)
        pairs = half(here) + 1
        span_all = [pl.ds(group * ROWS, ROWS) for group in range(GROUP)]

        def block_pair(pair, part):
            return blocks[head, pl.ds(2 * pair, 2), part].reshape(PAIR, HEAD_DIM)

        stats[0] = jnp.full((8, STACK), NEG_FILL, F32)
        for index in range(2):
            for group, span in enumerate(span_all):
                tile = (queries, grad_out)[index][0, 0, :, lanes(head * GROUP + group)]
                stacks[index, span, :] = tile
                turned[index, :, span] = tile.T

        @pl.loop(0, pairs)
        def _(pair):
            span_rows = rows_of(pair, PAIR)
            logits[span_rows, :] = jnp.dot(
                block_pair(pair, 0), turned[0], preferred_element_type=F32
            )
            grad_probs[span_rows, :] = jnp.dot(
                block_pair(pair, 1), turned[1], preferred_element_type=F32
            )

            @pl.when(pair == 0)
            def _():
                u_row = lax.broadcasted_iota(jnp.int32, (ROWS, ROWS), 0)
                t_row = lax.broadcasted_iota(jnp.int32, (ROWS, ROWS), 1)
                for span in span_all:
                    logits[0:ROWS, span] = jnp.where(
                        u_row <= t_row, logits[0:ROWS, span], NEG_FILL
                    )

            @pl.when((pair == pairs - 1) & (odd(here) == 0))
            def _():
                logits[rows_of(here + 1, ROWS), :] = jnp.full((ROWS, STACK), NEG_FILL, F32)

            for span in span_all:
                stats[0, :, span] = jnp.maximum(
                    stats[0, :, span], fold(logits[span_rows, span]).max(0)
                )

        stats[1] = jnp.zeros((8, STACK), F32)
        stats[2] = jnp.zeros((8, STACK), F32)
        stats[0] = jnp.broadcast_to(stats[0].max(0, keepdims=True), (8, STACK))

        @pl.loop(0, pairs)
        def _(pair):
            span_rows = rows_of(pair, PAIR)
            for span in span_all:
                top = stats[0, 0:1, span]
                tile = jnp.exp2((logits[span_rows, span] - top) * EXP2_SCALE)
                logits[span_rows, span] = tile
                stats[1, :, span] += fold(tile).sum(0)
                stats[2, :, span] += fold(tile * grad_probs[span_rows, span]).sum(0)

        inverse = 1.0 / stats[1].sum(0, keepdims=True)
        delta = stats[2].sum(0, keepdims=True) * inverse
        stats[1] = jnp.broadcast_to(inverse, (8, STACK))
        stats[2] = jnp.broadcast_to(delta, (8, STACK))
        query_sum[...] = jnp.zeros((HEAD_DIM, STACK), F32)

        @pl.loop(0, pairs)
        def _(pair):
            span_rows = rows_of(pair, PAIR)
            for span in span_all:
                exact = logits[span_rows, span] * stats[1, 0:1, span]
                probs[:, span] = exact.astype(BF16)
                grad_logits[:, span] = (
                    exact * (grad_probs[span_rows, span] - stats[2, 0:1, span])
                ).astype(BF16)
            value_term = jnp.dot(probs[...], stacks[1], preferred_element_type=F32)
            key_term = SCALE * jnp.dot(
                grad_logits[...], stacks[0], preferred_element_type=F32
            )
            for part, term in enumerate((key_term, value_term)):
                terms[head, pl.ds(2 * pair, 2), part] = term.astype(BF16).reshape(
                    2, ROWS, HEAD_DIM
                )

                @pl.when(pair == 0)
                def _():
                    own[head, part] = term[0:ROWS]

            query_sum[...] += lax.dot_general(
                block_pair(pair, 0), grad_logits[...], (((0,), (0,)), ((), ())),
                preferred_element_type=F32,
            )

        for group, span in enumerate(span_all):
            grad_queries[0, 0, :, lanes(head * GROUP + group)] = (SCALE * query_sum[:, span].T).astype(BF16)

    pl.loop(0, KV_HEADS)(attend)


def reduce_kernel(
    parents, terms, own, grad_kv,
    anc, spread, term_pieces,
    kept, total_sum, cross_out, cross_in, climb_out, climb_in, final_out, final_in,
    b1_send, b1_recv, x_send, x_recv, c_send, c_recv, f_send, f_recv,
):
    level, me, y, core = place()
    sibling = 2 * y + 1 - core
    enter()

    def send_terms(head):
        here = level

        def send(count):
            @pl.loop(1, SEGS)
            def _(step):
                peer = wrapped(me + step)
                part, span = piece_of(peer)
                remote(
                    terms.at[head, pl.ds(1, count), part, span, :],
                    term_pieces.at[head, pl.ds(1, count), me],
                    b1_send.at[head], b1_recv.at[head], (level, peer),
                ).start()

            part, span = piece_of(me)
            pltpu.make_async_copy(
                terms.at[head, pl.ds(1, count), part, span, :],
                term_pieces.at[head, pl.ds(1, count), me], b1_recv.at[head],
            ).start()

        per_plane(here, send)
    pl.loop(0, KV_HEADS)(send_terms)
    find_ancestors(parents, anc, level)
    make_spread(spread, anc, level)

    def summed(head, offset):
        return jnp.dot(
            spread[offset],
            term_pieces[head, offset].reshape(SEGS * PIECE, HEAD_DIM),
            preferred_element_type=F32,
        )

    def cross_copy(head, plane):
        return remote(
            cross_out.at[head, plane], cross_in.at[head, plane],
            x_send.at[head, plane], x_recv.at[head, plane], (sibling, me),
        )

    def sum_stage(head):
        here = host_of(head)

        def sums(count):
            wait_bytes(term_pieces.at[head, pl.ds(1, count)], b1_recv.at[head])
            for plane in range((count + 1) // 2):
                offset = jnp.maximum(here - (2 * plane + 1 - core), 1)
                cross_out[head, plane] = summed(head, offset).astype(BF16)
            for plane in range((count - 1) // 2):
                offset = jnp.maximum(here - (2 * plane + core), 1)
                kept[head, plane] = summed(head, offset)

        per_plane(here, sums)

        @pl.loop(0, 4)
        def _(plane):
            @pl.when(here - (2 * plane + 1 - core) >= 1)
            def _():
                cross_copy(head, plane).start()

    def climb_copy(head, plane):
        slot = half(host_of(head)) - 1
        return remote(
            climb_out.at[head, plane], climb_in.at[head, slot],
            c_send.at[head, plane], c_recv.at[head, slot], (device_of(head, plane), me),
        )

    def climb(head):
        plane_here = half(host_of(head))

        @pl.loop(0, plane_here - core + 1)
        def _(plane):
            wait_bytes(cross_in.at[head, plane], x_recv.at[head, plane])

        @pl.loop(0, plane_here)
        def _(plane):
            climb_out[head, plane] = (
                kept[head, plane] + cross_in[head, plane].astype(F32)
            ).astype(BF16)
            climb_copy(head, plane).start()

    def final_send(head):
        host = host_of(head)

        @pl.when(host < LEVELS - 1)
        def _():
            total_sum[...] = jnp.zeros((SEGS * PIECE, HEAD_DIM), F32)

            @pl.loop(half(host), 3)
            def _(slot):
                wait_bytes(climb_in.at[head, slot], c_recv.at[head, slot])
                total_sum[...] += climb_in[head, slot].astype(F32)

            @pl.when(core == 0)
            def _():
                total_sum[...] += cross_in[head, half(host)].astype(F32)

            final_out[head] = total_sum[...].astype(BF16).reshape(SEGS, PIECE, HEAD_DIM)
            part, span = piece_of(me)

            @pl.loop(1, SEGS)
            def _(step):
                peer = wrapped(me + step)
                remote(
                    final_out.at[head, peer], final_in.at[head, part, span, :],
                    f_send.at[head], f_recv.at[head], (host, peer),
                ).start()

            pltpu.make_async_copy(
                final_out.at[head, me], final_in.at[head, part, span, :], f_recv.at[head]
            ).start()

    def final_store(head):
        @pl.when(level < LEVELS - 1)
        def _():
            wait_bytes(final_in.at[head], f_recv.at[head])
            grad_kv[0, 0, :, :, lanes(head)] = (
                own[head] + final_in[head].astype(F32)
            ).astype(BF16)

        @pl.when(level == LEVELS - 1)
        def _():
            grad_kv[0, 0, :, :, lanes(head)] = own[head].astype(BF16)

    stages = (sum_stage, climb, final_send, final_store)

    @pl.loop(0, KV_HEADS + len(stages) - 1)
    def _(tick):
        for lag, stage in enumerate(stages):
            @pl.when((tick >= lag) & (tick < KV_HEADS + lag))
            def _():
                stage(tick - lag)

    @pl.loop(0, KV_HEADS)
    def _(head):
        per_plane(
            level,
            lambda count: wait_bytes(
                term_pieces.at[head, pl.ds(1, count), pl.ds(1, SEGS - 1)], b1_send.at[head]
            ),
        )

        @pl.loop(0, 4)
        def _(plane):
            @pl.when(level - (2 * plane + 1 - core) >= 1)
            def _():
                cross_copy(head, plane).wait_send()

        @pl.loop(0, half(level))
        def _(plane):
            climb_copy(head, plane).wait_send()

        @pl.when(level < LEVELS - 1)
        def _():
            wait_bytes(final_out.at[head, pl.ds(1, SEGS - 1)], f_send.at[head])


def shards(queries, keys_values, grad_out, parents):
    vmem = pl.BlockSpec(memory_space=pltpu.VMEM)
    smem = pl.BlockSpec(memory_space=pltpu.SMEM)
    dma = pltpu.SemaphoreType.DMA
    tile = (SEGS, PIECE, HEAD_DIM)
    flat = (SEGS * PIECE, HEAD_DIM)
    keys_count = LEVELS * ROWS
    part_pair = (2, ROWS, HEAD_DIM)
    selectors = (LEVELS, SEGS * PIECE, SEGS * PIECE)
    found = pltpu.SMEM((LEVELS, SEGS), jnp.int32)
    all_parts = jax.ShapeDtypeStruct((KV_HEADS, LEVELS) + part_pair, BF16)
    parent_rows = parents.transpose(0, 2, 1)

    def limits(**more):
        return pltpu.CompilerParams(vmem_limit_bytes=24 * 1024 * 1024, **more)

    blocks = pl.pallas_call(
        gather_kernel,
        out_shape=all_parts,
        in_specs=[smem, vmem],
        out_specs=vmem,
        scratch_shapes=[
            found,
            pltpu.VMEM(selectors, BF16),
            pltpu.VMEM((LEVELS, SEGS, PIECE, KV_HEADS * HEAD_DIM), BF16),
            pltpu.VMEM((KV_HEADS, SEGS, LEVELS - 1, PIECE, HEAD_DIM), BF16),
            dma, dma,
            dma((KV_HEADS, 7)), dma((KV_HEADS, LEVELS)),
            dma((KV_HEADS,)), dma((KV_HEADS,)),
        ],
        compiler_params=limits(collective_id=0, has_side_effects=True),
    )(parent_rows, keys_values)
    grad_queries, terms, own = pl.pallas_call(
        attend_kernel,
        out_shape=(
            jax.ShapeDtypeStruct(queries.shape, BF16),
            all_parts,
            jax.ShapeDtypeStruct((KV_HEADS,) + part_pair, F32),
        ),
        in_specs=[vmem, vmem, vmem],
        out_specs=(vmem, vmem, vmem),
        scratch_shapes=[
            pltpu.VMEM((2, STACK, HEAD_DIM), BF16),
            pltpu.VMEM((2, HEAD_DIM, STACK), BF16),
            pltpu.VMEM((HEAD_DIM, STACK), F32),
            pltpu.VMEM((3, 8, STACK), F32),
            pltpu.VMEM((keys_count, STACK), F32),
            pltpu.VMEM((keys_count, STACK), F32),
            pltpu.VMEM((PAIR, STACK), BF16),
            pltpu.VMEM((PAIR, STACK), BF16),
        ],
        compiler_params=limits(),
    )(blocks, queries, grad_out)
    grad_kv = pl.pallas_call(
        reduce_kernel,
        out_shape=jax.ShapeDtypeStruct(keys_values.shape, BF16),
        in_specs=[smem, vmem, vmem],
        out_specs=vmem,
        scratch_shapes=[
            found,
            pltpu.VMEM(selectors, BF16),
            pltpu.VMEM((KV_HEADS, LEVELS) + tile, BF16),
            pltpu.VMEM((KV_HEADS, 3) + flat, F32),
            pltpu.VMEM(flat, F32),
            pltpu.VMEM((KV_HEADS, 4) + flat, BF16),
            pltpu.VMEM((KV_HEADS, 4) + flat, BF16),
            pltpu.VMEM((KV_HEADS, 3) + flat, BF16),
            pltpu.VMEM((KV_HEADS, 3) + flat, BF16),
            pltpu.VMEM((KV_HEADS,) + tile, BF16),
            pltpu.VMEM((KV_HEADS,) + part_pair, BF16),
            dma((KV_HEADS,)), dma((KV_HEADS,)),
            dma((KV_HEADS, 4)), dma((KV_HEADS, 4)),
            dma((KV_HEADS, 3)), dma((KV_HEADS, 3)),
            dma((KV_HEADS,)), dma((KV_HEADS,)),
        ],
        compiler_params=limits(collective_id=1, has_side_effects=True),
    )(parent_rows, terms, own)
    return grad_queries, grad_kv


def solution(mesh):
    in_specs = (
        P("depth", "seg", None, None),
        P("depth", "seg", None, None, None),
        P("depth", "seg", None, None),
        P(),
    )
    out_specs = (P("depth", "seg", None, None), P("depth", "seg", None, None, None))
    return jax.shard_map(shards, mesh=mesh, in_specs=in_specs, out_specs=out_specs, check_vma=False)
```

time: 87.7 us -> 113 us (1.29)
  Pallas kernels: 84 us -> 110 us
    pallas_call x1 -> x3, Pallas kernels: 84 us -> 110 us  [the longest x1 78.9 us: shards(): pl.pallas_call(reduce_kernel, out_shape=jax.ShapeDtypeStruct(keys_values....]
    unnamed x4 -> x9, local copies, waits for them, and re-layouts: 2.71 us -> 2.44 us
where the time goes in v3:
time: 113 us
  Pallas kernels  110 us (97%)
  local copies, waits for them, and re-layouts  2.44 us (2%)
    pallas_call x1, Pallas kernels, shards(): pl.pallas_call(reduce_kernel, out_shape=jax.ShapeDtypeStruct(keys_values....  78.9 us
    pallas_call x1, Pallas kernels, shards(): pl.pallas_call(gather_kernel, out_shape=all_parts, in_specs=[smem, vmem],...  23.9 us
    pallas_call x1, Pallas kernels, shards(): pl.pallas_call(attend_kernel, out_shape=(jax.ShapeDtypeStruct(queries.sha...  7.28 us
    unnamed x9, local copies, waits for them, and re-layouts  2.44 us

profile of v3, /device:TPU:0, one launch (start us, length us, event | category | flops | bytes accessed | tf_op | source)
XLA Modules:
  0.0 113.2 jit_solution(1520410342804050813)
XLA Ops:
  0.6 0.0 copy-start.1
  0.6 0.0 copy-start
  0.7 0.0 copy-start.2
  0.7 1.0 copy-done.2
  1.7 0.0 copy-start.3
  1.7 0.7 copy-done.3
  2.4 23.9 %shard_map.59.blocks = bf16[4,8,2,128,128]{4,3,2,1,0:T(8,128)(2,1)S(1)} custom-call(s32[7,1,16]{2,1,0:T(1,128)S(1)} %bitcast.1, bf16[1,1,2,128,512]{4,3,2,1,0:T(8,128)(2,1)S(1)} %copy-done.2), custom_call_target="tpu_custom_call" | custom-call | tf_op jit(solution)/shard_map/pallas_call | solution.py:555
  26.3 0.0 copy-done.1
  26.3 0.0 copy-done
  26.3 7.3 %shard_map.60 = (bf16[1,1,128,2560]{3,2,1,0:T(8,128)(2,1)}, bf16[4,8,2,128,128]{4,3,2,1,0:T(8,128)(2,1)S(1)}, f32[4,2,128,128]{3,2,1,0:T(8,128)S(1)}) custom-call(bf16[4,8,2,128,128]{4,3,2,1,0:T(8,128)(2,1)S(1)} %shard_map.59.blocks, bf16[1,1,128,2560]{3,2,1,0:T(8,128)(2,1)S(1)} %copy-done, bf16[1,1,128,2560]{3,2,1,0:T(8,128)(2,1)S(1)} %copy-done.1), custom_call_target="tpu_custom_call" | custom-call | tf_op jit(solution)/shard_map/pallas_call | solution.py:571
  33.6 78.9 %shard_map.61 = bf16[1,1,2,128,512]{4,3,2,1,0:T(8,128)(2,1)S(1)} custom-call(s32[7,1,16]{2,1,0:T(1,128)S(1)} %bitcast.2, bf16[4,8,2,128,128]{4,3,2,1,0:T(8,128)(2,1)S(1)} %get-tuple-element.6.terms, f32[4,2,128,128]{3,2,1,0:T(8,128)S(1)} %get-tuple-element.7.own), custom_call_target="tpu_custom_call" | custom-call | tf_op jit(solution)/shard_map/pallas_call | solution.py:592
  112.5 0.7 copy.7
Async XLA Ops:
  0.6 25.7 %copy-start.1 = (bf16[1,1,128,2560]{3,2,1,0:T(8,128)(2,1)S(1)}, bf16[1,1,128,2560]{3,2,1,0:T(8,128)(2,1)}, u32[]{:S(2)}) copy-start(bf16[1,1,128,2560]{3,2,1,0:T(8,128)(2,1)} %grad_out.1) | copy-start | bytes 1966084
  0.6 25.7 %copy-start = (bf16[1,1,128,2560]{3,2,1,0:T(8,128)(2,1)S(1)}, bf16[1,1,128,2560]{3,2,1,0:T(8,128)(2,1)}, u32[]{:S(2)}) copy-start(bf16[1,1,128,2560]{3,2,1,0:T(8,128)(2,1)} %queries.1) | copy-start | bytes 1966084
  0.7 1.1 copy-start.2
  1.7 0.7 copy-start.3

commit v4 on v2

--- a/solution.py
+++ b/solution.py
@@ -18,8 +18,7 @@
 PIECES_PER_PART = ROWS // PIECE
 STACK = GROUP * ROWS
 PAIR = 2 * ROWS
-LAG = 2
-SWAPPED = 1
+LAG = 3
 
 NEG_FILL = -1e30
 SCALE = HEAD_DIM ** -0.5
@@ -37,16 +36,8 @@
     return lax.rem(value, 2)
 
 
-def is_swapped(head):
-    return head == SWAPPED
-
-
 def name_of(head):
-    return jnp.where(is_swapped(head), KV_HEADS - 1, head - jnp.where(head > SWAPPED, 1, 0))
-
-
-def group_of(head):
-    return jnp.where(is_swapped(head), 1, 0)
+    return 2 * odd(head) + half(head)
 
 
 def wrapped(index):
@@ -85,15 +76,13 @@
     y = half(level)
     core = odd(level)
     sibling = 2 * y + 1 - core
-    outer = (y == 0) | (y == 3)
-    partner = jnp.where(outer, 2 * (3 - y) + core, level)
+    partner = 2 * (3 - y) + core
 
     def host_of(head):
-        return jnp.where(is_swapped(head), partner, level)
+        return jnp.where(odd(head) == 1, partner, level)
 
     def device_of(head, plane):
-        swapped = is_swapped(head) & ((plane == 0) | (plane == 3))
-        return 2 * jnp.where(swapped, 3 - plane, plane) + core
+        return 2 * jnp.where(odd(head) == 1, 3 - plane, plane) + core
 
     def remote(src, dst, send_sem, recv_sem, device):
         return pltpu.make_async_remote_copy(
@@ -121,12 +110,6 @@
         def _():
             pltpu.make_async_copy(src, dst, recv_sem).start()
 
-    kept_width = (KV_HEADS - 1) * HEAD_DIM
-    spread_groups = (
-        (level, pl.ds(0, kept_width)),
-        (partner, pl.ds(kept_width, HEAD_DIM)),
-    )
-
     barrier = pltpu.get_barrier_semaphore()
 
     def greet(device):
@@ -140,39 +123,30 @@
     for step in range(1, 4):
         greet((lax.rem(level + 2 * step, LEVELS), me))
 
-    @pl.when(outer)
-    def _():
-        @pl.loop(0, SEGS)
-        def _(step):
-            greet((partner, wrapped(me + step)))
-
-    pl.semaphore_wait(barrier, SEGS - 1 + 4 + jnp.where(outer, SEGS, 0))
-
-    for group, (host, span_lanes) in enumerate(spread_groups):
+    @pl.loop(0, SEGS)
+    def _(step):
+        greet((partner, wrapped(me + step)))
+
+    pl.semaphore_wait(barrier, 2 * SEGS + 3)
+
+    def spread_out(head):
+        host = host_of(head)
+        span_lanes = lanes(name_of(head))
+
         def source(peer):
             part, span = piece_of(peer)
             return keys_values.at[0, 0, part, span, span_lanes]
 
-        def landing():
-            return pieces.at[level, me, :, span_lanes]
+        landing = pieces.at[level, me, :, span_lanes]
 
         @pl.loop(1, SEGS)
         def _(step):
             peer = wrapped(me + step)
             remote(
-                source(peer), landing(), p1_send.at[group], p1_recv.at[group], (host, peer)
+                source(peer), landing, p1_send.at[head], p1_recv.at[head], (host, peer)
             ).start()
 
-        if group == 1:
-            @pl.when(host != level)
-            def _():
-                remote(
-                    source(me), landing(), p1_send.at[group], p1_recv.at[group], (host, me)
-                ).start()
-
-        @pl.when(host == level)
-        def _():
-            pltpu.make_async_copy(source(me), landing(), p1_recv.at[group]).start()
+        move(head, source(me), landing, p1_send.at[head], p1_recv.at[head])
 
     def move_inputs(head):
         name = name_of(head)
@@ -198,34 +172,63 @@
     def own_lifts(head, action):
         here = host_of(head)
         plane = half(here)
-        for step in range(1, 4):
-            @pl.when(plane + step <= 3)
-            def _():
-                action(lift(head, here, step - 1, device_of(head, plane + step)))
+        routes = (
+            (plane <= 2, 0, plane + 1),
+            (plane == 0, 1, 3),
+            ((plane == 1) & (core == 1), 1, 0),
+        )
+        for condition, slot, target in routes:
+            @pl.when(condition)
+            def _():
+                action(lift(head, here, slot, device_of(head, target)))
 
         @pl.when(core == 0)
         def _():
-            action(lift(head, here, 3, sibling))
-
-    def passed_on(head, action):
-        @pl.loop(0, half(host_of(head)))
-        def _(plane):
-            action(2 * plane + core, lift(head, 2 * plane + core, 4 + plane, sibling))
-
-    for group, (host, span_lanes) in enumerate(spread_groups):
-        wait_bytes(pieces.at[host, :, :, span_lanes], p1_recv.at[group])
-
-    @pl.loop(0, KV_HEADS)
-    def _(head):
+            action(lift(head, here, 2, sibling))
+
+    relays = (
+        (0, 1, 1, 3),
+        (1, 0, 0, 2),
+        (2, 1, 0, 3),
+        (2, 0, None, None),
+        (3, 0, 1, 2),
+        (3, 2, None, None),
+        (3, 1, None, None),
+    )
+
+    def passed_on(head, before, action):
+        plane_here = half(host_of(head))
+        for plane, owner, relay_core, target in relays:
+            which = 2 * owner + core
+            needed = plane_here == plane
+            if plane < owner:
+                needed = needed & (core == relay_core)
+
+            @pl.when(needed)
+            def _():
+                before(which)
+                if target is not None:
+                    copy = lift(head, which, 3, device_of(head, target))
+                    if plane < owner:
+                        action(copy)
+                    else:
+                        pl.when(core == relay_core)(lambda: action(copy))
+                if plane > owner:
+                    action(lift(head, which, 4 + owner, sibling))
+
+    def launch(head):
+        wait_bytes(
+            pieces.at[host_of(head), :, :, lanes(name_of(head))], p1_recv.at[head]
+        )
         own_lifts(head, lambda copy: copy.start())
-
-    @pl.loop(0, KV_HEADS)
-    def _(head):
         move_inputs(head)
 
-    @pl.loop(0, 2)
-    def _(parity):
-        target_level = jnp.where(parity == 1, partner, level)
+    pl.loop(0, 2)(spread_out)
+    pl.loop(0, 2)(launch)
+    pl.loop(2, KV_HEADS)(spread_out)
+
+    def make_selectors(parity):
+        target_level = host_of(parity)
 
         @pl.loop(0, SEGS)
         def _(column):
@@ -251,6 +254,8 @@
                     target == row + column * PIECE, 1.0, 0.0
                 ).astype(BF16)
 
+    make_selectors(0)
+
     @pl.loop(0, KV_HEADS)
     def _(head):
         @pl.when(host_of(head) == 0)
@@ -258,15 +263,15 @@
             blocks[head, 1] = jnp.zeros((2, ROWS, HEAD_DIM), BF16)
 
     def pass_on(head):
-        def forward(which, copy):
-            wait_bytes(unit(head, which), up_recv.at[head, which])
-            copy.start()
-
-        passed_on(head, forward)
+        passed_on(
+            head,
+            lambda which: wait_bytes(unit(head, which), up_recv.at[head, which]),
+            lambda copy: copy.start(),
+        )
 
     def select(head):
         here = host_of(head)
-        parity = group_of(head)
+        parity = odd(head)
 
         @pl.loop(0, 4)
         def _(plane):
@@ -435,7 +440,7 @@
 
     def summed(head, offset):
         return jnp.dot(
-            spread[group_of(head), offset],
+            spread[odd(head), offset],
             term_pieces[head, offset].reshape(SEGS * PIECE, HEAD_DIM),
             preferred_element_type=F32,
         )
@@ -538,13 +543,21 @@
 
     @pl.loop(0, KV_HEADS + LAG + len(stages))
     def _(tick):
+        @pl.when((tick >= 1) & (tick < KV_HEADS + 1))
+        def _():
+            select(tick - 1)
+
         @pl.when(tick < KV_HEADS)
         def _():
             pass_on(tick)
 
-        @pl.when((tick >= 1) & (tick < KV_HEADS + 1))
-        def _():
-            select(tick - 1)
+        @pl.when(tick < KV_HEADS - 2)
+        def _():
+            launch(tick + 2)
+
+        @pl.when(tick == 0)
+        def _():
+            make_selectors(1)
 
         @pl.when((tick >= LAG) & (tick < KV_HEADS + LAG))
         def _():
@@ -562,24 +575,19 @@
             @pl.when((tick >= lag) & (tick < KV_HEADS + lag))
             def _():
                 stage(tick - lag)
-
-    for group, (host, span_lanes) in enumerate(spread_groups):
-        wait_bytes(pieces.at[0, pl.ds(1, SEGS - 1), :, span_lanes], p1_send.at[group])
-        if group == 1:
-            @pl.when(host != level)
-            def _():
-                wait_bytes(pieces.at[0, 0, :, span_lanes], p1_send.at[group])
 
     @pl.loop(0, KV_HEADS)
     def _(head):
         host = host_of(head)
         away = host != level
         wait_bytes(query_target(head), d_recv.at[head])
+        wait_bytes(final_out.at[head, pl.ds(1, SEGS - 1)], p1_send.at[head])
         own_lifts(head, lambda copy: copy.wait_send())
-        passed_on(head, lambda which, copy: copy.wait_send())
+        passed_on(head, lambda which: None, lambda copy: copy.wait_send())
 
         @pl.when(away)
         def _():
+            wait_bytes(final_out.at[head, 0], p1_send.at[head])
             wait_bytes(blocks.at[head, 0], k_send.at[head])
             wait_bytes(inputs.at[head], q_send.at[head])
             wait_bytes(staged.at[head], d_send.at[head])
@@ -652,7 +660,7 @@
         pltpu.VMEM((KV_HEADS, 3) + flat, BF16),
         pltpu.VMEM((KV_HEADS,) + tile, BF16),
         pltpu.VMEM((KV_HEADS,) + part_pair, BF16),
-        dma((2,)), dma((2,)),
+        dma((KV_HEADS,)), dma((KV_HEADS,)),
         dma((KV_HEADS, 7)), dma((KV_HEADS, LEVELS)),
         dma((KV_HEADS,)), dma((KV_HEADS,)),
         dma((KV_HEADS,)), dma((KV_HEADS,)),

time: 87.7 us -> 94.1 us (1.073)
  Pallas kernels: 84 us -> 90.6 us
    pallas_call x1, Pallas kernels: 84 us -> 90.6 us  [shards(): pl.pallas_call(kernel, out_shape=(jax.ShapeDtypeStruct(queries.shape, BF1...]
where the time goes in v4:
time: 94.1 us; the launch traced here: 94 us
  Pallas kernels  90.6 us (96%)
  local copies, waits for them, and re-layouts  2.71 us (3%)
    pallas_call x1, Pallas kernels, shards(): pl.pallas_call(kernel, out_shape=(jax.ShapeDtypeStruct(queries.shape, BF1...  90.6 us
    unnamed x4, local copies, waits for them, and re-layouts  2.71 us

profile of v4, /device:TPU:0, one launch (start us, length us, event | category | flops | bytes accessed | tf_op | source)
XLA Modules:
  0.0 94.0 jit_solution(4411907273162560808)
XLA Ops:
  0.6 90.6 %shard_map.59 = (bf16[1,1,128,2560]{3,2,1,0:T(8,128)(2,1)}, bf16[1,1,2,128,512]{4,3,2,1,0:T(8,128)(2,1)}) custom-call(s32[7,1,16]{2,1,0:T(1,128)} %bitcast.1, bf16[1,1,128,2560]{3,2,1,0:T(8,128)(2,1)} %queries.1, bf16[1,1,2,128,512]{4,3,2,1,0:T(8,128)(2,1)} %keys_values.1, bf16[1,1,128,2560]{3,2,1,0:T(8,128)(2,1)} %grad_out.1), custom_call_target="tpu_custom_call" | custom-call | flops 3355443200 | bytes 8388608 | tf_op jit(solution)/shard_map/pallas_call | solution.py:675
  91.2 0.0 copy-start
  91.3 2.0 %copy.8 = bf16[1,1,128,2560]{3,2,1,0:T(8,128)(2,1)} copy(bf16[1,1,128,2560]{3,2,1,0:T(8,128)(2,1)} %get-tuple-element.4) | data formatting | bytes 1310720
  93.3 0.0 copy-done
  93.3 0.7 copy.9
Async XLA Ops:
  91.2 2.0 %copy-start = (bf16[1,1,2,128,512]{4,3,2,1,0:T(8,128)(2,1)S(1)}, bf16[1,1,2,128,512]{4,3,2,1,0:T(8,128)(2,1)}, u32[]{:S(2)}) copy-start(bf16[1,1,2,128,512]{4,3,2,1,0:T(8,128)(2,1)} %get-tuple-element.5) | copy-start | bytes 786436

commit v5 on v4

--- a/solution.py
+++ b/solution.py
@@ -76,13 +76,15 @@
     y = half(level)
     core = odd(level)
     sibling = 2 * y + 1 - core
-    partner = 2 * (3 - y) + core
+    outer = (y == 0) | (y == 3)
+    partner = jnp.where(outer, 2 * (3 - y) + core, level)
 
     def host_of(head):
         return jnp.where(odd(head) == 1, partner, level)
 
     def device_of(head, plane):
-        return 2 * jnp.where(odd(head) == 1, 3 - plane, plane) + core
+        swapped = (odd(head) == 1) & ((plane == 0) | (plane == 3))
+        return 2 * jnp.where(swapped, 3 - plane, plane) + core
 
     def remote(src, dst, send_sem, recv_sem, device):
         return pltpu.make_async_remote_copy(
@@ -123,11 +125,13 @@
     for step in range(1, 4):
         greet((lax.rem(level + 2 * step, LEVELS), me))
 
-    @pl.loop(0, SEGS)
-    def _(step):
-        greet((partner, wrapped(me + step)))
-
-    pl.semaphore_wait(barrier, 2 * SEGS + 3)
+    @pl.when(outer)
+    def _():
+        @pl.loop(0, SEGS)
+        def _(step):
+            greet((partner, wrapped(me + step)))
+
+    pl.semaphore_wait(barrier, SEGS + 3 + jnp.where(outer, SEGS, 0))
 
     def spread_out(head):
         host = host_of(head)
@@ -172,10 +176,14 @@
     def own_lifts(head, action):
         here = host_of(head)
         plane = half(here)
+        plain = odd(head) == 0
         routes = (
-            (plane <= 2, 0, plane + 1),
-            (plane == 0, 1, 3),
-            ((plane == 1) & (core == 1), 1, 0),
+            (plain & (plane <= 2), 0, plane + 1),
+            (plain & (plane == 0), 1, 3),
+            (plain & (plane == 1) & (core == 1), 1, 0),
+            ((~plain) & (plane <= 1), 0, 2),
+            ((~plain) & (plane <= 1), 1, 3),
+            ((~plain) & (plane == 2), 0, 1 - core),
         )
         for condition, slot, target in routes:
             @pl.when(condition)
@@ -187,20 +195,28 @@
             action(lift(head, here, 2, sibling))
 
     relays = (
-        (0, 1, 1, 3),
-        (1, 0, 0, 2),
-        (2, 1, 0, 3),
-        (2, 0, None, None),
-        (3, 0, 1, 2),
-        (3, 2, None, None),
-        (3, 1, None, None),
+        (0, 0, 1, 1, 3),
+        (0, 1, 0, 0, 2),
+        (0, 2, 1, 0, 3),
+        (0, 2, 0, None, None),
+        (0, 3, 0, 1, 2),
+        (0, 3, 2, None, None),
+        (0, 3, 1, None, None),
+        (1, 0, 2, 1, 3),
+        (1, 1, 2, 0, 3),
+        (1, 1, 0, None, None),
+        (1, 2, 0, 0, 1),
+        (1, 2, 1, None, None),
+        (1, 3, 0, 1, 1),
+        (1, 3, 1, None, None),
+        (1, 3, 2, None, None),
     )
 
     def passed_on(head, before, action):
         plane_here = half(host_of(head))
-        for plane, owner, relay_core, target in relays:
+        for parity, plane, owner, relay_core, target in relays:
             which = 2 * owner + core
-            needed = plane_here == plane
+            needed = (plane_here == plane) & (odd(head) == parity)
             if plane < owner:
                 needed = needed & (core == relay_core)
 
@@ -221,7 +237,6 @@
             pieces.at[host_of(head), :, :, lanes(name_of(head))], p1_recv.at[head]
         )
         own_lifts(head, lambda copy: copy.start())
-        move_inputs(head)
 
     pl.loop(0, 2)(spread_out)
     pl.loop(0, 2)(launch)
@@ -558,6 +573,13 @@
         @pl.when(tick == 0)
         def _():
             make_selectors(1)
+            move_inputs(0)
+            move_inputs(2)
+
+        @pl.when(tick == KV_HEADS - 1)
+        def _():
+            move_inputs(1)
+            move_inputs(3)
 
         @pl.when((tick >= LAG) & (tick < KV_HEADS + LAG))
         def _():

time: 94.1 us -> 86.9 us (0.923)
  Pallas kernels: 90.6 us -> 83.3 us
    pallas_call x1, Pallas kernels: 90.6 us -> 83.3 us  [shards(): pl.pallas_call(kernel, out_shape=(jax.ShapeDtypeStruct(queries.shape, BF1...]
where the time goes in v5:
time: 86.9 us; the launch traced here: 86.7 us
  Pallas kernels  83.3 us (96%)
  local copies, waits for them, and re-layouts  2.71 us (3%)
    pallas_call x1, Pallas kernels, shards(): pl.pallas_call(kernel, out_shape=(jax.ShapeDtypeStruct(queries.shape, BF1...  83.3 us
    unnamed x4, local copies, waits for them, and re-layouts  2.71 us

profile of v5, /device:TPU:0, one launch (start us, length us, event | category | flops | bytes accessed | tf_op | source)
XLA Modules:
  0.0 86.7 jit_solution(17803778983639531941)
XLA Ops:
  0.6 83.3 %shard_map.59 = (bf16[1,1,128,2560]{3,2,1,0:T(8,128)(2,1)}, bf16[1,1,2,128,512]{4,3,2,1,0:T(8,128)(2,1)}) custom-call(s32[7,1,16]{2,1,0:T(1,128)} %bitcast.1, bf16[1,1,128,2560]{3,2,1,0:T(8,128)(2,1)} %queries.1, bf16[1,1,2,128,512]{4,3,2,1,0:T(8,128)(2,1)} %keys_values.1, bf16[1,1,128,2560]{3,2,1,0:T(8,128)(2,1)} %grad_out.1), custom_call_target="tpu_custom_call" | custom-call | flops 3355443200 | bytes 8388608 | tf_op jit(solution)/shard_map/pallas_call | solution.py:697
  84.0 0.0 copy-start
  84.0 2.0 %copy.8 = bf16[1,1,128,2560]{3,2,1,0:T(8,128)(2,1)} copy(bf16[1,1,128,2560]{3,2,1,0:T(8,128)(2,1)} %get-tuple-element.4) | data formatting | bytes 1310720
  86.0 0.0 copy-done
  86.0 0.7 copy.9
Async XLA Ops:
  84.0 2.0 %copy-start = (bf16[1,1,2,128,512]{4,3,2,1,0:T(8,128)(2,1)S(1)}, bf16[1,1,2,128,512]{4,3,2,1,0:T(8,128)(2,1)}, u32[]{:S(2)}) copy-start(bf16[1,1,2,128,512]{4,3,2,1,0:T(8,128)(2,1)} %get-tuple-element.5) | copy-start | bytes 786436

commit v6 on v1

--- a/solution.py
+++ b/solution.py
@@ -18,7 +18,7 @@
 PIECES_PER_PART = ROWS // PIECE
 STACK = GROUP * ROWS
 PAIR = 2 * ROWS
-LAG = 2
+LAG = 3
 
 NEG_FILL = -1e30
 SCALE = HEAD_DIM ** -0.5
@@ -112,6 +112,43 @@
         def _():
             pltpu.make_async_copy(src, dst, recv_sem).start()
 
+    def find_ancestors(parity):
+        target_level = host_of(parity)
+
+        @pl.loop(0, SEGS)
+        def _(column):
+            current = column
+            for offset in range(1, LEVELS):
+                current = parents[jnp.maximum(target_level - offset, 0), 0, current]
+                anc[parity, offset, column] = current
+
+    def make_pick(parity):
+        @pl.loop(1, 2 * half(host_of(parity)) + 2)
+        def _(offset):
+            lane = lax.broadcasted_iota(jnp.int32, (PIECE, SEGS * PIECE), 1)
+            row = lax.broadcasted_iota(jnp.int32, (PIECE, SEGS * PIECE), 0)
+            ahead = lane - row
+            for column in range(SEGS):
+                pick[parity, offset, rows_of(column, PIECE), :] = jnp.where(
+                    ahead == anc[parity, offset, column] * PIECE, 1.0, 0.0
+                ).astype(BF16)
+
+    def make_spread(parity):
+        @pl.loop(1, 2 * half(host_of(parity)) + 2)
+        def _(offset):
+            lane = lax.broadcasted_iota(jnp.int32, (PIECE, SEGS * PIECE), 1)
+            row = lax.broadcasted_iota(jnp.int32, (PIECE, SEGS * PIECE), 0)
+            lane_column = lane >> 4
+            target = (lane & (PIECE - 1)) - row
+            for column in range(SEGS):
+                target = jnp.where(
+                    lane_column == column, target + anc[parity, offset, column] * PIECE, target
+                )
+            for column in range(SEGS):
+                spread[parity, offset, rows_of(column, PIECE), :] = jnp.where(
+                    target == column * PIECE, 1.0, 0.0
+                ).astype(BF16)
+
     barrier = pltpu.get_barrier_semaphore()
 
     def greet(device):
@@ -131,6 +168,7 @@
         def _(step):
             greet((partner, wrapped(me + step)))
 
+    find_ancestors(0)
     pl.semaphore_wait(barrier, SEGS - 1 + 4 + jnp.where(outer, SEGS, 0))
 
     @pl.loop(0, 2)
@@ -200,41 +238,15 @@
         def _(plane):
             action(2 * plane + core, lift(head, 2 * plane + core, 4 + plane, sibling))
 
-    for group in range(2):
-        here = host_of(group)
-        wait_bytes(pieces.at[group, here], p1_recv.at[group])
-        own_lifts(group, lambda copy: copy.start())
-        move_inputs(group)
-        own_lifts(group + 2, lambda copy: copy.start())
-        move_inputs(group + 2)
-
-    @pl.loop(0, 2)
-    def _(parity):
-        target_level = host_of(parity)
-
-        @pl.loop(0, SEGS)
-        def _(column):
-            current = column
-            for offset in range(1, LEVELS):
-                current = parents[jnp.maximum(target_level - offset, 0), 0, current]
-                anc[parity, offset, column] = current
-
-        @pl.loop(1, 2 * half(target_level) + 2)
-        def _(offset):
-            lane = lax.broadcasted_iota(jnp.int32, (PIECE, SEGS * PIECE), 1)
-            row = lax.broadcasted_iota(jnp.int32, (PIECE, SEGS * PIECE), 0)
-            target = lane % PIECE
-            lane_column = lane // PIECE
-            for column in range(SEGS):
-                found = anc[parity, offset, column] * PIECE
-                pick[parity, offset, rows_of(column, PIECE), :] = jnp.where(
-                    lane == found + row, 1.0, 0.0
-                ).astype(BF16)
-                target = target + jnp.where(lane_column == column, found, 0)
-            for column in range(SEGS):
-                spread[parity, offset, rows_of(column, PIECE), :] = jnp.where(
-                    target == row + column * PIECE, 1.0, 0.0
-                ).astype(BF16)
+    def launch(head):
+        @pl.when(head < 2)
+        def _():
+            wait_bytes(pieces.at[head, host_of(head)], p1_recv.at[head])
+
+        own_lifts(head, lambda copy: copy.start())
+
+    make_pick(0)
+    launch(0)
 
     @pl.loop(0, KV_HEADS)
     def _(head):
@@ -522,13 +534,39 @@
 
     @pl.loop(0, KV_HEADS + LAG + len(stages))
     def _(tick):
+        @pl.when((tick >= 1) & (tick < KV_HEADS + 1))
+        def _():
+            select(tick - 1)
+
+        @pl.when(tick < KV_HEADS - 1)
+        def _():
+            launch(tick + 1)
+
         @pl.when(tick < KV_HEADS)
         def _():
             pass_on(tick)
 
-        @pl.when((tick >= 1) & (tick < KV_HEADS + 1))
-        def _():
-            select(tick - 1)
+        @pl.when(tick == 0)
+        def _():
+            find_ancestors(1)
+            make_pick(1)
+
+        @pl.when(tick == 2)
+        def _():
+            move_inputs(0)
+            move_inputs(2)
+            make_spread(0)
+            make_spread(1)
+
+        @pl.when(tick == 3)
+        def _():
+            move_inputs(1)
+            move_inputs(3)
+
+        for lag, stage in reversed(list(enumerate(stages[1:], LAG + 2))):
+            @pl.when((tick >= lag) & (tick < KV_HEADS + lag))
+            def _():
+                stage(tick - lag)
 
         @pl.when((tick >= LAG) & (tick < KV_HEADS + LAG))
         def _():
@@ -542,10 +580,9 @@
             attend(head)
             send_results(head)
 
-        for lag, stage in enumerate(stages, LAG + 1):
-            @pl.when((tick >= lag) & (tick < KV_HEADS + lag))
-            def _():
-                stage(tick - lag)
+        @pl.when((tick >= LAG + 1) & (tick < KV_HEADS + LAG + 1))
+        def _():
+            sum_stage(tick - LAG - 1)
 
     @pl.loop(0, 2)
     def _(group):

time: 82.5 us -> 86.7 us (1.051)
  Pallas kernels: 78.8 us -> 83.2 us
    pallas_call x1, Pallas kernels: 78.8 us -> 83.2 us  [shards(): pl.pallas_call(kernel, out_shape=(jax.ShapeDtypeStruct(queries.shape, BF1...]
where the time goes in v6:
time: 86.7 us; the launch traced here: 86.6 us
  Pallas kernels  83.2 us (96%)
  local copies, waits for them, and re-layouts  2.71 us (3%)
    pallas_call x1, Pallas kernels, shards(): pl.pallas_call(kernel, out_shape=(jax.ShapeDtypeStruct(queries.shape, BF1...  83.2 us
    unnamed x4, local copies, waits for them, and re-layouts  2.71 us

profile of v6, /device:TPU:0, one launch (start us, length us, event | category | flops | bytes accessed | tf_op | source)
XLA Modules:
  0.0 86.6 jit_solution(7626099839602898473)
XLA Ops:
  0.6 83.2 %shard_map.59 = (bf16[1,1,128,2560]{3,2,1,0:T(8,128)(2,1)}, bf16[1,1,2,128,512]{4,3,2,1,0:T(8,128)(2,1)}) custom-call(s32[7,1,16]{2,1,0:T(1,128)} %bitcast.1, bf16[1,1,128,2560]{3,2,1,0:T(8,128)(2,1)} %queries.1, bf16[1,1,2,128,512]{4,3,2,1,0:T(8,128)(2,1)} %keys_values.1, bf16[1,1,128,2560]{3,2,1,0:T(8,128)(2,1)} %grad_out.1), custom_call_target="tpu_custom_call" | custom-call | flops 3355443200 | bytes 8388608 | tf_op jit(solution)/shard_map/pallas_call | solution.py:688
  83.9 0.0 copy-start
  83.9 2.0 %copy.8 = bf16[1,1,128,2560]{3,2,1,0:T(8,128)(2,1)} copy(bf16[1,1,128,2560]{3,2,1,0:T(8,128)(2,1)} %get-tuple-element.4) | data formatting | bytes 1310720
  85.9 0.0 copy-done
  85.9 0.7 copy.9
Async XLA Ops:
  83.9 2.0 %copy-start = (bf16[1,1,2,128,512]{4,3,2,1,0:T(8,128)(2,1)S(1)}, bf16[1,1,2,128,512]{4,3,2,1,0:T(8,128)(2,1)}, u32[]{:S(2)}) copy-start(bf16[1,1,2,128,512]{4,3,2,1,0:T(8,128)(2,1)} %get-tuple-element.5) | copy-start | bytes 786436

commit v7 on v6

--- a/solution.py
+++ b/solution.py
@@ -18,7 +18,7 @@
 PIECES_PER_PART = ROWS // PIECE
 STACK = GROUP * ROWS
 PAIR = 2 * ROWS
-LAG = 3
+LAG = 2
 
 NEG_FILL = -1e30
 SCALE = HEAD_DIM ** -0.5
@@ -244,6 +244,7 @@
             wait_bytes(pieces.at[head, host_of(head)], p1_recv.at[head])
 
         own_lifts(head, lambda copy: copy.start())
+        move_inputs(head)
 
     make_pick(0)
     launch(0)
@@ -553,15 +554,8 @@
 
         @pl.when(tick == 2)
         def _():
-            move_inputs(0)
-            move_inputs(2)
             make_spread(0)
             make_spread(1)
-
-        @pl.when(tick == 3)
-        def _():
-            move_inputs(1)
-            move_inputs(3)
 
         for lag, stage in reversed(list(enumerate(stages[1:], LAG + 2))):
             @pl.when((tick >= lag) & (tick < KV_HEADS + lag))

time: 86.7 us -> 84.9 us (0.979)
  Pallas kernels: 83.2 us -> 81.4 us
    pallas_call x1, Pallas kernels: 83.2 us -> 81.4 us  [shards(): pl.pallas_call(kernel, out_shape=(jax.ShapeDtypeStruct(queries.shape, BF1...]
where the time goes in v7:
time: 84.9 us; the launch traced here: 84.7 us
  Pallas kernels  81.4 us (96%)
  local copies, waits for them, and re-layouts  2.71 us (3%)
    pallas_call x1, Pallas kernels, shards(): pl.pallas_call(kernel, out_shape=(jax.ShapeDtypeStruct(queries.shape, BF1...  81.4 us
    unnamed x4, local copies, waits for them, and re-layouts  2.71 us

profile of v7, /device:TPU:0, one launch (start us, length us, event | category | flops | bytes accessed | tf_op | source)
XLA Modules:
  0.0 84.7 jit_solution(2014739035811343459)
XLA Ops:
  0.6 81.4 %shard_map.59 = (bf16[1,1,128,2560]{3,2,1,0:T(8,128)(2,1)}, bf16[1,1,2,128,512]{4,3,2,1,0:T(8,128)(2,1)}) custom-call(s32[7,1,16]{2,1,0:T(1,128)} %bitcast.1, bf16[1,1,128,2560]{3,2,1,0:T(8,128)(2,1)} %queries.1, bf16[1,1,2,128,512]{4,3,2,1,0:T(8,128)(2,1)} %keys_values.1, bf16[1,1,128,2560]{3,2,1,0:T(8,128)(2,1)} %grad_out.1), custom_call_target="tpu_custom_call" | custom-call | flops 3355443200 | bytes 8388608 | tf_op jit(solution)/shard_map/pallas_call | solution.py:682
  82.0 0.0 copy-start
  82.0 2.0 %copy.8 = bf16[1,1,128,2560]{3,2,1,0:T(8,128)(2,1)} copy(bf16[1,1,128,2560]{3,2,1,0:T(8,128)(2,1)} %get-tuple-element.4) | data formatting | bytes 1310720
  84.0 0.0 copy-done
  84.0 0.7 copy.9
Async XLA Ops:
  82.0 2.0 %copy-start = (bf16[1,1,2,128,512]{4,3,2,1,0:T(8,128)(2,1)S(1)}, bf16[1,1,2,128,512]{4,3,2,1,0:T(8,128)(2,1)}, u32[]{:S(2)}) copy-start(bf16[1,1,2,128,512]{4,3,2,1,0:T(8,128)(2,1)} %get-tuple-element.5) | copy-start | bytes 786436

commit v8 on v7

--- a/solution.py
+++ b/solution.py
@@ -64,10 +64,11 @@
 
 def kernel(
     parents, queries, keys_values, grad_out, grad_queries, grad_kv,
-    anc, pick, spread, pieces, chosen, blocks, terms, term_pieces, own, own_out, own_in,
+    anc, pick, spread, kv_in, kv_stage, pieces, chosen, blocks, own_blocks, whole,
+    terms, term_pieces, own, own_out, own_in,
     inputs, stacks, staged, query_sum, stats, logits, grad_probs, probs, grad_logits,
     kept, total_sum, cross_out, cross_in, climb_out, climb_in, final_out, final_in,
-    p1_send, p1_recv, up_send, up_recv, q_send, q_recv, k_send, k_recv, p3_send, p3_recv,
+    kv_sem, p1_send, p1_recv, up_send, up_recv, q_send, q_recv, k_send, k_recv, p3_send, p3_recv,
     b1_send, b1_recv, o_send, o_recv, d_send, d_recv, x_send, x_recv, c_send, c_recv,
     f_send, f_recv,
 ):
@@ -154,6 +155,9 @@
     def greet(device):
         pl.semaphore_signal(barrier, inc=1, device_id=device, device_id_type=MESH)
 
+    load = pltpu.make_async_copy(keys_values, kv_in, kv_sem)
+    load.start()
+
     @pl.loop(1, SEGS)
     def _(step):
         greet((level, wrapped(me + step)))
@@ -169,41 +173,35 @@
             greet((partner, wrapped(me + step)))
 
     find_ancestors(0)
+    load.wait()
+    for name in range(KV_HEADS):
+        for part in range(2):
+            kv_stage[name, pl.ds(part * PIECES_PER_PART, PIECES_PER_PART)] = kv_in[
+                0, 0, part, :, name * HEAD_DIM:(name + 1) * HEAD_DIM
+            ].reshape(PIECES_PER_PART, PIECE, HEAD_DIM)
     pl.semaphore_wait(barrier, SEGS - 1 + 4 + jnp.where(outer, SEGS, 0))
 
     @pl.loop(0, 2)
     def _(group):
         host = host_of(group)
 
-        def source(peer):
-            part, span = piece_of(peer)
-            return keys_values.at[0, 0, part, span, lanes(group, 2)]
+        names = pl.ds(2 * group, 2)
+        landing = pieces.at[names, level, me]
 
         @pl.loop(1, SEGS)
         def _(step):
             peer = wrapped(me + step)
             remote(
-                source(peer), pieces.at[group, level, me],
+                kv_stage.at[names, peer], landing,
                 p1_send.at[group], p1_recv.at[group], (host, peer),
             ).start()
 
-        @pl.when(host != level)
-        def _():
-            remote(
-                source(me), pieces.at[group, level, me],
-                p1_send.at[group], p1_recv.at[group], (host, me),
-            ).start()
-
-        @pl.when(host == level)
-        def _():
-            pltpu.make_async_copy(
-                source(me), pieces.at[group, level, me], p1_recv.at[group]
-            ).start()
+        move(group, kv_stage.at[names, me], landing, p1_send.at[group], p1_recv.at[group])
 
     def move_inputs(head):
         name = name_of(head)
         move(
-            head, keys_values.at[0, 0, :, :, lanes(name)], blocks.at[head, 0],
+            head, kv_stage.at[name], own_blocks.at[head],
             k_send.at[head], k_recv.at[head],
         )
         for index, array in enumerate((queries, grad_out)):
@@ -213,7 +211,7 @@
             )
 
     def unit(head, which):
-        return pieces.at[odd(head), which, :, :, lanes(half(head))]
+        return pieces.at[name_of(head), which]
 
     def lift(head, which, slot, device):
         return remote(
@@ -241,19 +239,13 @@
     def launch(head):
         @pl.when(head < 2)
         def _():
-            wait_bytes(pieces.at[head, host_of(head)], p1_recv.at[head])
+            wait_bytes(pieces.at[pl.ds(2 * head, 2), host_of(head)], p1_recv.at[head])
 
         own_lifts(head, lambda copy: copy.start())
         move_inputs(head)
 
     make_pick(0)
     launch(0)
-
-    @pl.loop(0, KV_HEADS)
-    def _(head):
-        @pl.when(host_of(head) == 0)
-        def _():
-            blocks[head, 1] = jnp.zeros((2, ROWS, HEAD_DIM), BF16)
 
     def pass_on(head):
         def forward(which, copy):
@@ -278,26 +270,24 @@
             for offset in range(1, count + 1):
                 found = jnp.dot(
                     pick[parity, offset],
-                    pieces[
-                        parity, jnp.maximum(here - offset, 0), :, :, lanes(half(head))
-                    ].reshape(SEGS * PIECE, HEAD_DIM),
+                    pieces[name_of(head), jnp.maximum(here - offset, 0)].reshape(
+                        SEGS * PIECE, HEAD_DIM
+                    ),
                     preferred_element_type=F32,
                 )
                 chosen[head, :, offset - 1] = found.astype(BF16).reshape(SEGS, PIECE, HEAD_DIM)
-            part, span = piece_of(me)
-
             @pl.loop(1, SEGS)
             def _(step):
                 peer = wrapped(me + step)
                 remote(
                     chosen.at[head, peer, pl.ds(0, count)],
-                    blocks.at[head, pl.ds(1, count), part, span, :],
+                    blocks.at[head, me, pl.ds(0, count)],
                     p3_send.at[head], p3_recv.at[head], (level, peer),
                 ).start()
 
             pltpu.make_async_copy(
                 chosen.at[head, me, pl.ds(0, count)],
-                blocks.at[head, pl.ds(1, count), part, span, :], p3_recv.at[head],
+                blocks.at[head, me, pl.ds(0, count)], p3_recv.at[head],
             ).start()
 
         per_plane(here, send)
@@ -309,7 +299,24 @@
         span_all = [pl.ds(group * ROWS, ROWS) for group in range(GROUP)]
 
         def block_pair(pair, part):
-            return blocks[head, pl.ds(2 * pair, 2), part].reshape(PAIR, HEAD_DIM)
+            return whole[part, rows_of(pair, PAIR), :]
+
+        halves = [pl.ds(part * PIECES_PER_PART, PIECES_PER_PART) for part in range(2)]
+        for part, span in enumerate(halves):
+            whole[part, 0:ROWS, :] = own_blocks[head, span].reshape(ROWS, HEAD_DIM)
+
+        @pl.when(here == 0)
+        def _():
+            whole[:, ROWS:PAIR, :] = jnp.zeros((2, ROWS, HEAD_DIM), BF16)
+
+        @pl.when(here > 0)
+        def _():
+            @pl.loop(1, 2 * pairs)
+            def _(offset):
+                for part, span in enumerate(halves):
+                    whole[part, rows_of(offset, ROWS), :] = blocks[
+                        head, span, offset - 1
+                    ].reshape(ROWS, HEAD_DIM)
 
         stats[0] = jnp.full((8, STACK), NEG_FILL, F32)
         for index in range(2):
@@ -378,9 +385,9 @@
                 grad_logits[...], stacks[0], preferred_element_type=F32
             )
             for part, term in enumerate((key_term, value_term)):
-                terms[head, pl.ds(2 * pair, 2), part] = term.astype(BF16).reshape(
-                    2, ROWS, HEAD_DIM
-                )
+                cut = term.astype(BF16).reshape(2, PIECES_PER_PART, PIECE, HEAD_DIM)
+                for index in range(2):
+                    terms[head, halves[part], 2 * pair + index] = cut[index]
 
                 @pl.when(pair == 0)
                 def _():
@@ -405,17 +412,15 @@
             @pl.loop(1, SEGS)
             def _(step):
                 peer = wrapped(me + step)
-                part, span = piece_of(peer)
                 remote(
-                    terms.at[head, pl.ds(1, count), part, span, :],
-                    term_pieces.at[head, pl.ds(1, count), me],
+                    terms.at[head, peer, pl.ds(1, count)],
+                    term_pieces.at[head, me, pl.ds(0, count)],
                     b1_send.at[head], b1_recv.at[head], (level, peer),
                 ).start()
 
-            part, span = piece_of(me)
             pltpu.make_async_copy(
-                terms.at[head, pl.ds(1, count), part, span, :],
-                term_pieces.at[head, pl.ds(1, count), me], b1_recv.at[head],
+                terms.at[head, me, pl.ds(1, count)],
+                term_pieces.at[head, me, pl.ds(0, count)], b1_recv.at[head],
             ).start()
 
         per_plane(here, send)
@@ -433,7 +438,7 @@
     def summed(head, offset):
         return jnp.dot(
             spread[odd(head), offset],
-            term_pieces[head, offset].reshape(SEGS * PIECE, HEAD_DIM),
+            term_pieces[head, :, offset - 1].reshape(SEGS * PIECE, HEAD_DIM),
             preferred_element_type=F32,
         )
 
@@ -447,7 +452,7 @@
         here = host_of(head)
 
         def sums(count):
-            wait_bytes(term_pieces.at[head, pl.ds(1, count)], b1_recv.at[head])
+            wait_bytes(term_pieces.at[head, :, pl.ds(0, count)], b1_recv.at[head])
             for plane in range((count + 1) // 2):
                 offset = jnp.maximum(here - (2 * plane + 1 - core), 1)
                 cross_out[head, plane] = summed(head, offset).astype(BF16)
@@ -567,9 +572,9 @@
             head = tick - LAG
             per_plane(
                 host_of(head),
-                lambda count: wait_bytes(blocks.at[head, pl.ds(1, count)], p3_recv.at[head]),
-            )
-            wait_bytes(blocks.at[head, 0], k_recv.at[head])
+                lambda count: wait_bytes(blocks.at[head, :, pl.ds(0, count)], p3_recv.at[head]),
+            )
+            wait_bytes(own_blocks.at[head], k_recv.at[head])
             wait_bytes(inputs.at[head], q_recv.at[head])
             attend(head)
             send_results(head)
@@ -580,11 +585,12 @@
 
     @pl.loop(0, 2)
     def _(group):
-        wait_bytes(pieces.at[group, 0, pl.ds(1, SEGS - 1)], p1_send.at[group])
+        names = pl.ds(2 * group, 2)
+        wait_bytes(pieces.at[names, 0, pl.ds(1, SEGS - 1)], p1_send.at[group])
 
         @pl.when(host_of(group) != level)
         def _():
-            wait_bytes(pieces.at[group, 0, 0], p1_send.at[group])
+            wait_bytes(pieces.at[names, 0, 0], p1_send.at[group])
 
     @pl.loop(0, KV_HEADS)
     def _(head):
@@ -596,7 +602,7 @@
 
         @pl.when(away)
         def _():
-            wait_bytes(blocks.at[head, 0], k_send.at[head])
+            wait_bytes(own_blocks.at[head], k_send.at[head])
             wait_bytes(inputs.at[head], q_send.at[head])
             wait_bytes(staged.at[head], d_send.at[head])
             wait_bytes(own_out.at[head], o_send.at[head])
@@ -604,7 +610,7 @@
         def sent(count):
             wait_bytes(chosen.at[head, pl.ds(1, SEGS - 1), pl.ds(0, count)], p3_send.at[head])
             wait_bytes(
-                term_pieces.at[head, pl.ds(1, count), pl.ds(1, SEGS - 1)], b1_send.at[head]
+                term_pieces.at[head, pl.ds(1, SEGS - 1), pl.ds(0, count)], b1_send.at[head]
             )
 
         per_plane(host, sent)
@@ -642,11 +648,15 @@
         pltpu.SMEM((2, LEVELS, SEGS), jnp.int32),
         pltpu.VMEM(selectors, BF16),
         pltpu.VMEM(selectors, BF16),
-        pltpu.VMEM((2, LEVELS, SEGS, PIECE, 2 * HEAD_DIM), BF16),
+        pltpu.VMEM(keys_values.shape, BF16),
+        pltpu.VMEM((KV_HEADS,) + tile, BF16),
+        pltpu.VMEM((KV_HEADS, LEVELS) + tile, BF16),
         pltpu.VMEM((KV_HEADS, SEGS, LEVELS - 1, PIECE, HEAD_DIM), BF16),
-        pltpu.VMEM((KV_HEADS, LEVELS) + part_pair, BF16),
-        pltpu.VMEM((KV_HEADS, LEVELS) + part_pair, BF16),
-        pltpu.VMEM((KV_HEADS, LEVELS) + tile, BF16),
+        pltpu.VMEM((KV_HEADS, SEGS, LEVELS - 1, PIECE, HEAD_DIM), BF16),
+        pltpu.VMEM((KV_HEADS,) + tile, BF16),
+        pltpu.VMEM((2, keys_count, HEAD_DIM), BF16),
+        pltpu.VMEM((KV_HEADS, SEGS, LEVELS, PIECE, HEAD_DIM), BF16),
+        pltpu.VMEM((KV_HEADS, SEGS, LEVELS - 1, PIECE, HEAD_DIM), BF16),
         pltpu.VMEM((KV_HEADS,) + part_pair, F32),
         pltpu.VMEM((KV_HEADS,) + part_pair, BF16),
         pltpu.VMEM((KV_HEADS,) + part_pair, BF16),
@@ -667,6 +677,7 @@
         pltpu.VMEM((KV_HEADS, 3) + flat, BF16),
         pltpu.VMEM((KV_HEADS,) + tile, BF16),
         pltpu.VMEM((KV_HEADS,) + part_pair, BF16),
+        dma,
         dma((2,)), dma((2,)),
         dma((KV_HEADS, 7)), dma((KV_HEADS, LEVELS)),
         dma((KV_HEADS,)), dma((KV_HEADS,)),

time: 84.9 us -> 84.8 us (level)
  no operation moved by 1% of the time
where the time goes in v8:
time: 84.8 us; the launch traced here: 84.7 us
  Pallas kernels  81.3 us (96%)
  local copies, waits for them, and re-layouts  2.71 us (3%)
    pallas_call x1, Pallas kernels, shards(): pl.pallas_call(kernel, out_shape=(jax.ShapeDtypeStruct(queries.shape, BF1...  81.3 us
    unnamed x4, local copies, waits for them, and re-layouts  2.71 us

profile of v8, /device:TPU:0, one launch (start us, length us, event | category | flops | bytes accessed | tf_op | source)
XLA Modules:
  0.0 84.7 jit_solution(9586065373308031497)
XLA Ops:
  0.6 81.3 %shard_map.59 = (bf16[1,1,128,2560]{3,2,1,0:T(8,128)(2,1)}, bf16[1,1,2,128,512]{4,3,2,1,0:T(8,128)(2,1)}) custom-call(s32[7,1,16]{2,1,0:T(1,128)} %bitcast.1, bf16[1,1,128,2560]{3,2,1,0:T(8,128)(2,1)} %queries.1, bf16[1,1,2,128,512]{4,3,2,1,0:T(8,128)(2,1)} %keys_values.1, bf16[1,1,128,2560]{3,2,1,0:T(8,128)(2,1)} %grad_out.1), custom_call_target="tpu_custom_call" | custom-call | flops 3355443200 | bytes 8388608 | tf_op jit(solution)/shard_map/pallas_call | solution.py:693
  81.9 0.0 copy-start
  81.9 2.0 %copy.8 = bf16[1,1,128,2560]{3,2,1,0:T(8,128)(2,1)} copy(bf16[1,1,128,2560]{3,2,1,0:T(8,128)(2,1)} %get-tuple-element.4) | data formatting | bytes 1310720
  84.0 0.0 copy-done
  84.0 0.7 copy.9
Async XLA Ops:
  81.9 2.0 %copy-start = (bf16[1,1,2,128,512]{4,3,2,1,0:T(8,128)(2,1)S(1)}, bf16[1,1,2,128,512]{4,3,2,1,0:T(8,128)(2,1)}, u32[]{:S(2)}) copy-start(bf16[1,1,2,128,512]{4,3,2,1,0:T(8,128)(2,1)} %get-tuple-element.5) | copy-start | bytes 786436
